TPU v7x, 32 devices: a whole 2x2x4 slice. The times are simulated.
32 devices in a mesh: gy: 8 (over z, core), gx: 4 (over y, x).
Axes of the slice: x: 2, y: 2, z: 4, core: 2. Of those that a mesh axis runs over, the one named last changes fastest.
Arguments:
- tokens: bfloat16 [256, 512, 256], P('gy', 'gx'), may hold values from -40 to 40
- cotangent: bfloat16 [256, 512, 256], P('gy', 'gx'), may hold values from -6 to 6
- norm1_gain: float32 [256], replicated, may hold values from 0.25 to 1.75
- w_qkv: bfloat16 [256, 768], replicated, may hold values from -0.375 to 0.375
- w_out: bfloat16 [256, 256], replicated, may hold values from -0.375 to 0.375
- pos_bias: float32 [8, 64, 64], replicated, may hold values from -3.5 to 302
- norm2_gain: float32 [256], replicated, may hold values from 0.25 to 1.75
- w_up: bfloat16 [256, 1024], replicated, may hold values from -0.375 to 0.375
- w_down: bfloat16 [1024, 256], replicated, may hold values from -0.1875 to 0.1875
Outputs:
- mixed: bfloat16 [256, 512, 256], P('gy', 'gx')
- grad_tokens: bfloat16 [256, 512, 256], P('gy', 'gx')
- grad_qkv: float32 [256, 768], replicated
- grad_out: float32 [256, 256], replicated
All inputs are finite; a program needn't handle non-finite values.
Results may differ from a plain program's by a relative error of at most 0.009.
Values may be sent and summed in bfloat16 or wider, within the bound.
A program may use at most 192 MiB of HBM per device.

v0:
```python
import math

import jax
import jax.numpy as jnp
from jax import lax
from jax.sharding import PartitionSpec as P

GRID = 8


EPSILON = 1e-05


def normalize(values, gain):
    wide = values.astype(jnp.float32)
    centre = jnp.mean(wide, axis=-1, keepdims=True)
    shifted = wide - centre
    variance = jnp.mean(shifted * shifted, axis=-1, keepdims=True)
    inverse = lax.rsqrt(variance + EPSILON)
    unit = shifted * inverse
    return (unit * gain, unit, inverse)


def geometry(tile_rows, tile_cols, row_devices, column_devices):
    row_part = tile_rows // row_devices
    row_extra = row_devices // GRID
    local_members = GRID // column_devices
    strip_part = tile_cols // local_members // column_devices
    return (row_devices, row_part, row_extra, local_members, column_devices, strip_part)


def outbound(stacked, layout):
    row_devices, row_part, row_extra, local_members, column_devices, strip_part = layout
    return stacked.reshape(
        stacked.shape[0],
        row_devices,
        row_part,
        local_members,
        column_devices,
        strip_part,
        stacked.shape[-1],
    )


def inbound(received, layout):
    row_devices, row_part, row_extra, local_members, column_devices, strip_part = layout
    arranged = received.reshape(
        received.shape[0],
        GRID,
        row_extra,
        row_part,
        local_members,
        column_devices,
        strip_part,
        received.shape[-1],
    )
    arranged = arranged.transpose(0, 2, 3, 6, 1, 5, 4, 7)
    return arranged.reshape(received.shape[0], -1, received.shape[-1])


def homeward(flat, layout):
    row_devices, row_part, row_extra, local_members, column_devices, strip_part = layout
    arranged = flat.reshape(
        flat.shape[0],
        row_extra,
        row_part,
        strip_part,
        GRID,
        column_devices,
        local_members,
        flat.shape[-1],
    )
    arranged = arranged.transpose(0, 4, 1, 2, 6, 5, 3, 7)
    return arranged.reshape(
        flat.shape[0],
        row_devices,
        row_part,
        local_members,
        column_devices,
        strip_part,
        flat.shape[-1],
    )


def feed_forward(attended, norm2_gain, w_up, w_down):
    normed_wide, unit, inverse = normalize(attended, norm2_gain)
    normed2 = normed_wide.astype(jnp.bfloat16)
    hidden = jax.nn.gelu(jnp.dot(normed2, w_up, preferred_element_type=jnp.float32)).astype(
        jnp.bfloat16
    )
    return (
        attended.astype(jnp.float32) + jnp.dot(hidden, w_down, preferred_element_type=jnp.float32)
    ).astype(jnp.bfloat16)


def attention_forward(x_rows, norm1_gain, w_qkv, w_out, pos_bias):
    channels = x_rows.shape[-1]
    heads = pos_bias.shape[0]
    members = pos_bias.shape[1]
    width = channels // heads
    groups = x_rows.shape[0] // members
    scale_factor = 1.0 / math.sqrt(width)
    normed_wide, unit, inverse = normalize(x_rows, norm1_gain)
    normed = normed_wide.astype(jnp.bfloat16)
    qkv = jnp.dot(normed, w_qkv, preferred_element_type=jnp.float32).astype(jnp.bfloat16)
    split_qkv = qkv.reshape(groups, members, 3, heads, width)
    query = split_qkv[:, :, 0]
    keys = split_qkv[:, :, 1]
    values = split_qkv[:, :, 2]
    scores = (
        jnp.einsum("nmhd,nkhd->nhmk", query, keys, preferred_element_type=jnp.float32)
        * scale_factor
        + pos_bias[None]
    )
    soft = jax.nn.softmax(scores, axis=-1)
    soft_low = soft.astype(jnp.bfloat16)
    context = jnp.einsum("nhmk,nkhd->nmhd", soft_low, values, preferred_element_type=jnp.float32)
    context = context.astype(jnp.bfloat16).reshape(groups * members, channels)
    attended = (
        x_rows.astype(jnp.float32) + jnp.dot(context, w_out, preferred_element_type=jnp.float32)
    ).astype(jnp.bfloat16)
    saved = (normed, unit, inverse, query, keys, values, soft, soft_low, context)
    return (attended, saved)


def attention_backward(saved, g_rows, norm1_gain, w_qkv, w_out):
    normed, unit, inverse, query, keys, values, soft, soft_low, context = saved
    groups, members, heads, width = query.shape
    channels = heads * width
    scale_factor = 1.0 / math.sqrt(width)
    d_context = jnp.dot(g_rows, w_out.T, preferred_element_type=jnp.float32).astype(jnp.bfloat16)
    d_wout = lax.dot_general(
        context, g_rows, (((0,), (0,)), ((), ())), preferred_element_type=jnp.float32
    )
    d_ctx = d_context.reshape(groups, members, heads, width)
    d_soft = jnp.einsum("nmhd,nkhd->nhmk", d_ctx, values, preferred_element_type=jnp.float32)
    d_scores = soft * (d_soft - jnp.sum(soft * d_soft, axis=-1, keepdims=True))
    d_scaled = (d_scores * scale_factor).astype(jnp.bfloat16)
    d_query = jnp.einsum("nhmk,nkhd->nmhd", d_scaled, keys, preferred_element_type=jnp.float32)
    d_keys = jnp.einsum("nhmk,nmhd->nkhd", d_scaled, query, preferred_element_type=jnp.float32)
    d_values = jnp.einsum("nhmk,nmhd->nkhd", soft_low, d_ctx, preferred_element_type=jnp.float32)
    d_qkv = (
        jnp.stack([d_query, d_keys, d_values], axis=2)
        .astype(jnp.bfloat16)
        .reshape(groups * members, 3 * channels)
    )
    d_wqkv = lax.dot_general(
        normed, d_qkv, (((0,), (0,)), ((), ())), preferred_element_type=jnp.float32
    )
    d_normed = jnp.dot(d_qkv, w_qkv.T, preferred_element_type=jnp.float32)
    d_unit = d_normed * norm1_gain
    d_x = inverse * (
        d_unit
        - jnp.mean(d_unit, axis=-1, keepdims=True)
        - unit * jnp.mean(d_unit * unit, axis=-1, keepdims=True)
    )
    grad_rows = (g_rows.astype(jnp.float32) + d_x).astype(jnp.bfloat16)
    return (grad_rows, d_wqkv, d_wout)


def local(tokens, cotangent, norm1_gain, w_qkv, w_out, pos_bias, norm2_gain, w_up, w_down):
    tile_rows, tile_cols, channels = tokens.shape
    row_devices = lax.axis_size("gy")
    column_devices = lax.axis_size("gx")
    layout = geometry(tile_rows, tile_cols, row_devices, column_devices)
    factor = 1.0 / math.sqrt(tile_rows * tile_cols * row_devices * column_devices)
    sent = lax.all_to_all(
        lax.all_to_all(
            outbound(jnp.stack([tokens, cotangent]), layout),
            "gy",
            split_axis=1,
            concat_axis=1,
            tiled=True,
        ),
        "gx",
        split_axis=4,
        concat_axis=4,
        tiled=True,
    )
    grouped = inbound(sent, layout)
    x_rows = grouped[0]
    g_rows = grouped[1]
    attended, saved = attention_forward(x_rows, norm1_gain, w_qkv, w_out, pos_bias)
    grad_rows, d_wqkv, d_wout = attention_backward(saved, g_rows, norm1_gain, w_qkv, w_out)
    mixed_rows = feed_forward(attended, norm2_gain, w_up, w_down)
    returned = lax.all_to_all(
        lax.all_to_all(
            homeward(jnp.stack([mixed_rows, grad_rows]), layout),
            "gy",
            split_axis=1,
            concat_axis=1,
            tiled=True,
        ),
        "gx",
        split_axis=4,
        concat_axis=4,
        tiled=True,
    )
    tiles = returned.reshape(2, tile_rows, tile_cols, channels)
    mixed = tiles[0]
    grad_tokens = tiles[1]
    totals = lax.psum((d_wqkv, d_wout), ("gy", "gx"))
    return (mixed, grad_tokens, totals[0] * factor, totals[1] * factor)


def solution(mesh):
    placed = (P("gy", "gx", None), P("gy", "gx", None), P(), P(), P(), P(), P(), P(), P())
    return jax.shard_map(
        local,
        mesh=mesh,
        in_specs=placed,
        out_specs=(P("gy", "gx", None), P("gy", "gx", None), P(), P()),
        check_vma=False,
    )
```

profile of v0, /device:TPU:25, one launch (start us, length us, event | category | flops | bytes accessed | tf_op | source)
XLA Modules:
  0.0 793.5 jit_solution(5278972900159269503)
XLA Ops:
  7.2 4.6 pad_maximum_fusion
  11.8 6.5 copy.150
  18.3 96.7 %all_to_all.20 = bf16[2,8,4,2,4,16,256]{6,3,4,5,2,0,1:T(2,128)(2,1)} all-to-all(bf16[2,8,4,2,4,16,256]{6,3,4,5,2,0,1:T(2,128)(2,1)S(1)} %copy.150), channel_id=1, replica_groups=mesh['gy'=8,'gx'=4] {'gy'}, dimensions={1} | all-to-all | bytes 8388608 | tf_op jit(solution)/shard_map/all_to_all | solution.py:168
  115.0 8.5 %copy.151 = bf16[2,8,4,2,4,16,256]{6,3,1,5,2,0,4:T(2,128)(2,1)} copy(bf16[2,8,4,2,4,16,256]{6,3,4,5,2,0,1:T(2,128)(2,1)} %all_to_all.20) | data formatting | bytes 8388608 | tf_op jit(solution)/shard_map/all_to_all | solution.py:168
  123.5 5.1 all-to-all-start.1
  128.8 46.9 %all-to-all-done.1 = bf16[2,8,4,2,4,16,256]{6,3,1,5,2,0,4:T(2,128)(2,1)} async-done(((bf16[2,8,4,2,4,16,256]{6,3,1,5,2,0,4:T(2,128)(2,1)}), bf16[2,8,4,2,4,16,256]{6,3,1,5,2,0,4:T(2,128)(2,1)}, u32[]{:S(2)}, u32[]{:S(2)}) %all-to-all-start.1) | async-done | bytes 4194336 | tf_op jit(solution)/shard_map/all_to_all | solution.py:167
  175.7 3.2 copy.220
  179.0 0.9 convert_reduce_fusion.1
  179.8 1.2 copy-done.2
  181.0 2.7 slice_convert_fusion
  183.8 0.2 copy.157
  184.1 1.9 copy.156
  186.0 2.7 multiply_reduce_fusion.2
  188.6 0.8 copy.159
  189.4 0.9 add_rsqrt_fusion
  190.4 1.9 copy.160
  192.3 2.1 rsqrt.21
  194.4 6.4 copy.153
  200.9 6.1 reshape.139
  207.0 2.1 div.29
  209.1 5.9 convolution_convert_fusion
  215.0 8.7 %copy.161 = bf16[4096,768]{0,1:T(8,128)(2,1)} copy(bf16[4096,768]{1,0:T(8,128)(2,1)} %convolution_convert_fusion) | data formatting | bytes 12582912 | tf_op jit(solution)/shard_map/convert_element_type | solution.py:105
  223.8 18.0 %reshape.135 = bf16[64,64,3,8,32]{1,0,4,3,2:T(8,128)(2,1)} reshape(bf16[4096,768]{0,1:T(8,128)(2,1)} %copy.161) | data formatting | bytes 12582912 | tf_op jit(solution)/shard_map/reshape | solution.py:106
  241.7 9.8 %fusion.79 = (bf16[64,64,1,8,32]{1,0,4,3,2:T(8,128)(2,1)}, bf16[64,64,1,8,32]{1,0,4,3,2:T(8,128)(2,1)}, bf16[64,64,1,8,32]{1,0,4,3,2:T(8,128)(2,1)}) fusion(bf16[64,64,3,8,32]{1,0,4,3,2:T(8,128)(2,1)} %reshape.135), kind=kLoop, calls=%fused_computation.90 | loop fusion | bytes 12582912 | tf_op jit(solution)/shard_map/slice | solution.py:109
  251.5 3.5 copy.168
  255.0 2.7 squeeze.22
  257.8 2.1 convolution_convert_fusion.1
  259.9 4.1 copy.169
  263.9 6.9 reshape.137
  270.9 20.4 %fusion.42 = f32[64,8,64,64]{2,3,1,0:T(8,128)} fusion(bf16[64,64,1,8,32]{1,0,4,3,2:T(8,128)(2,1)} %get-tuple-element.9, bf16[64,64,1,8,32]{1,0,4,3,2:T(8,128)(2,1)} %get-tuple-element.10), kind=kOutput, calls=%fused_computation.58 | convolution fusion | flops 134217728 | bytes 12582912 | tf_op jit(solution)/shard_map/nmhd,nkhd->nhmk/dot_general | solution.py:111
  291.2 17.8 %fusion.81 = (f32[64,8,64]{2,1,0:T(8,128)S(1)}, f32[64,8,64,64]{2,3,1,0:T(8,128)}) fusion(f32[64,8,64,64]{2,3,1,0:T(8,128)} %fusion.42, f32[8,64,64]{1,2,0:T(8,128)S(1)} %copy.165), kind=kOutput, calls=%fused_computation.92 | output fusion | flops 12582975 | bytes 17039360 | tf_op jit(solution)/shard_map/sub | solution.py:115
  309.1 20.4 %fusion.41 = f32[64,8,64,64]{2,3,1,0:T(8,128)} fusion(bf16[64,64,1,8,32]{1,0,4,3,2:T(8,128)(2,1)} %get-tuple-element.8, bf16[64,64,8,32]{1,0,3,2:T(8,128)(2,1)} %reshape.137), kind=kOutput, calls=%fused_computation.57 | convolution fusion | flops 134217728 | bytes 12582912 | tf_op jit(solution)/shard_map/nmhd,nkhd->nhmk/dot_general | solution.py:136
  329.4 31.0 %fusion.50 = bf16[64,64,1,8,32]{1,4,3,0,2:T(8,128)(2,1)} fusion(f32[64,8,64,64]{2,3,1,0:T(8,128)} %fusion.41, bf16[64,64,1,8,32]{1,0,4,3,2:T(8,128)(2,1)} %get-tuple-element.10, f32[64,8,64,64]{2,3,1,0:T(8,128)} %get-tuple-element.16, f32[64,8,64]{2,1,0:T(8,128)S(1)} %get-tuple-element.15), kind=kOutput, calls=%fused_computation.62 | convolution fusion | flops 148930624 | bytes 21102592 | tf_op jit(solution)/shard_map/nhmk,nkhd->nmhd/dot_general | solution.py:139
  360.4 28.6 %fusion.53 = bf16[64,64,1,8,32]{1,4,3,0,2:T(8,128)(2,1)} fusion(f32[64,8,64,64]{2,3,1,0:T(8,128)} %fusion.41, bf16[64,64,1,8,32]{1,0,4,3,2:T(8,128)(2,1)} %get-tuple-element.9, f32[64,8,64,64]{2,3,1,0:T(8,128)} %get-tuple-element.16, f32[64,8,64]{2,1,0:T(8,128)S(1)} %get-tuple-element.15), kind=kOutput, calls=%fused_computation.63 | convolution fusion | flops 148930624 | bytes 21102592 | tf_op jit(solution)/shard_map/nhmk,nmhd->nkhd/dot_general | solution.py:140
  389.1 11.3 %fusion.45 = bf16[64,64,1,8,32]{1,4,3,0,2:T(8,128)(2,1)} fusion(bf16[64,64,8,32]{1,0,3,2:T(8,128)(2,1)} %reshape.137, f32[64,8,64,64]{2,3,1,0:T(8,128)} %get-tuple-element.16, f32[64,8,64]{2,1,0:T(8,128)S(1)} %get-tuple-element.15), kind=kOutput, calls=%fused_computation.61 | convolution fusion | flops 138412032 | bytes 12713984 | tf_op jit(solution)/shard_map/nhmk,nmhd->nkhd/dot_general | solution.py:141
  400.4 18.0 %convert_bitcast_fusion = bf16[64,64,8,32]{1,3,2,0:T(8,128)(2,1)} fusion(bf16[64,64,1,8,32]{1,0,4,3,2:T(8,128)(2,1)} %get-tuple-element.8, f32[64,8,64,64]{2,3,1,0:T(8,128)} %get-tuple-element.16, f32[64,8,64]{2,1,0:T(8,128)S(1)} %get-tuple-element.15), kind=kOutput, calls=%fused_computation.49 | convolution fusion | flops 139460608 | bytes 12713984 | tf_op jit(solution)/shard_map/nhmk,nkhd->nmhd/dot_general | solution.py:117
  418.4 7.4 maximum_convert_fusion
  425.8 9.3 %copy.175 = bf16[64,64,3,8,32]{1,0,4,3,2:T(8,128)(2,1)} copy(bf16[64,64,3,8,32]{1,4,3,0,2:T(8,128)(2,1)S(1)} %maximum_convert_fusion) | data formatting | bytes 12582912 | tf_op jit(solution)/shard_map/convert_element_type | solution.py:144
  435.1 17.2 %convert_element_type.91 = bf16[4096,768]{0,1:T(8,128)(2,1)} reshape(bf16[64,64,3,8,32]{1,0,4,3,2:T(8,128)(2,1)} %copy.175) | data formatting | bytes 12582912 | tf_op jit(solution)/shard_map/convert_element_type | solution.py:144
  452.2 6.8 copy.167
  459.1 5.7 reshape.136
  464.8 4.3 convert_reduce_fusion
  469.1 1.3 copy-done.6
  470.4 1.3 fusion.34
  471.8 9.1 %fusion.27 = bf16[4096,256]{1,0:T(8,128)(2,1)S(1)} fusion(bf16[1024,256]{1,0:T(8,128)(2,1)S(1)} %copy-done, bf16[4096,256]{1,0:T(8,128)(2,1)} %copy-done.6, bf16[256,1024]{1,0:T(8,128)(2,1)S(1)} %copy-done.21, f32[256]{0:T(256)S(1)} %copy-done.22, f32[4096]{0:T(1024)S(1)} %add_rsqrt_fusion.1, f32[4096]{0:T(1024)S(1)} %broadcast_multiply_fusion.5), kind=kOutput, calls=%fused_computation.32 | convolution fusion | flops 4341104640 | bytes 5276672 | tf_op jit(solution)/shard_map/dot_general | solution.py:92
  480.9 2.3 stack.33
  483.2 8.6 %fusion.78 = (f32[4096]{0:T(1024)S(1)}, f32[4096]{0:T(1024)S(1)}, f32[4096,256]{1,0:T(8,128)S(1)}) fusion(f32[4096]{0:T(1024)S(1)} %copy-done.15, f32[4096,256]{1,0:T(8,128)} %reshape.139, f32[4096]{0:T(1024)S(1)} %copy-done.17, f32[256]{0:T(256)S(1)} %copy-done.20, bf16[4096,768]{0,1:T(8,128)(2,1)} %convert_element_type.91, bf16[256,768]{1,0:T(8,128)(2,1)S(1)} %copy-done.13), kind=kOutput, calls=%fused_computation.89 | convolution fusion | flops 1616896000 | bytes 15139840 | tf_op jit(solution)/shard_map/dot_general | solution.py:150
  491.9 4.4 add_convert_fusion
  496.2 4.1 stack.38
  500.3 6.6 copy_bitcast_fusion.3
  506.9 97.5 %all_to_all.21 = bf16[2,8,4,2,4,16,256]{6,3,4,5,2,0,1:T(2,128)(2,1)} all-to-all(bf16[2,8,4,2,4,16,256]{6,3,4,5,2,0,1:T(2,128)(2,1)S(1)} %copy_bitcast_fusion.3), channel_id=1, replica_groups=mesh['gy'=8,'gx'=4] {'gy'}, dimensions={1} | all-to-all | bytes 8388608 | tf_op jit(solution)/shard_map/all_to_all | solution.py:187
  604.5 8.5 %copy.178 = bf16[2,8,4,2,4,16,256]{6,3,1,5,2,0,4:T(2,128)(2,1)} copy(bf16[2,8,4,2,4,16,256]{6,3,4,5,2,0,1:T(2,128)(2,1)} %all_to_all.21) | data formatting | bytes 8388608 | tf_op jit(solution)/shard_map/all_to_all | solution.py:187
  613.0 5.0 all-to-all-start.3
  618.2 2.7 multiply_convert_fusion.1
  621.0 3.5 copy.182
  624.5 4.1 convert_element_type.94
  628.6 3.1 fusion.83
  631.8 5.6 fusion.82
  637.4 136.4 %all-reduce.3.cloned.1.call-done = (f32[256,768]{1,0:T(8,128)}, f32[256,256]{1,0:T(8,128)}) async-done(((f32[256,768]{1,0:T(8,128)}, f32[256,256]{1,0:T(8,128)}), (f32[256,768]{1,0:T(8,128)}, f32[256,256]{1,0:T(8,128)})) %all-reduce.3.cloned.1.call-update) | async-done | bytes 1048592 | tf_op jit(solution)/shard_map/psum | solution.py:202
  773.8 1.7 broadcast_multiply_fusion.1
  775.5 2.1 broadcast_multiply_fusion
  777.6 4.8 fusion.80
  782.4 2.0 copy.193
  784.4 2.0 copy.194
  (54 shorter events, 0.7 us)
Async XLA Ops:
  7.2 464.6 %copy-start = (bf16[1024,256]{1,0:T(8,128)(2,1)S(1)}, bf16[1024,256]{1,0:T(8,128)(2,1)}, u32[]{:S(2)}) copy-start(bf16[1024,256]{1,0:T(8,128)(2,1)} %param.17) | copy-start | bytes 1572868
  123.5 5.2 copy-start.18
  123.5 52.2 %all-to-all-start.1 = ((bf16[2,8,4,2,4,16,256]{6,3,1,5,2,0,4:T(2,128)(2,1)}), bf16[2,8,4,2,4,16,256]{6,3,1,5,2,0,4:T(2,128)(2,1)}, u32[]{:S(2)}, u32[]{:S(2)}) async-start(bf16[2,8,4,2,4,16,256]{6,3,1,5,2,0,4:T(2,128)(2,1)} %copy.151), calls=%async_computation.1 | async-start | bytes 8388608 | tf_op jit(solution)/shard_map/all_to_all | solution.py:167
  179.0 2.1 copy-start.2
  184.0 16.8 %copy-start.7 = (f32[4,16,8,4,2]{2,4,3,1,0:T(2,128)}, f32[4,16,8,4,2]{2,4,3,1,0:T(2,128)S(1)}, u32[]{:S(2)}) copy-start(f32[4,16,8,4,2]{2,4,3,1,0:T(2,128)S(1)} %copy.157) | copy-start | bytes 49156
  190.4 10.5 %copy-start.10 = (f32[4,16,8,4,2]{1,2,4,3,0:T(8,128)}, f32[4,16,8,4,2]{1,2,4,3,0:T(8,128)S(1)}, u32[]{:S(2)}) copy-start(f32[4,16,8,4,2]{1,2,4,3,0:T(8,128)S(1)} %add_rsqrt_fusion) | copy-start | bytes 49156
  194.4 14.7 %copy-start.14 = (f32[4096]{0:T(1024)}, f32[4096]{0:T(1024)S(1)}, u32[]{:S(2)}) copy-start(f32[4096]{0:T(1024)S(1)} %rsqrt.21) | copy-start | bytes 49156
  200.9 8.2 %copy-start.19 = (f32[256]{0:T(256)S(1)}, f32[256]{0:T(256)}, u32[]{:S(2)}) copy-start(f32[256]{0:T(256)} %param.11) | copy-start | bytes 3076
  209.1 5.9 copy-start.16
  251.5 6.3 copy-start.12
  257.8 6.1 copy-start.3
  464.7 4.3 copy-start.5
  464.8 7.0 copy-start.21
  464.8 7.0 copy-start.22
  469.1 1.3 copy-start.6
  480.9 2.3 copy-start.13
  480.9 2.3 copy-start.15
  480.9 2.3 copy-start.17
  480.9 2.3 copy-start.20
  483.2 8.7 %copy-start.1 = (f32[4096,256]{1,0:T(8,128)S(1)}, f32[4096,256]{1,0:T(8,128)}, u32[]{:S(2)}) copy-start(f32[4096,256]{1,0:T(8,128)} %reshape.139) | copy-start | bytes 12582916
  483.2 8.7 %copy-start.4 = (bf16[4096,256]{1,0:T(8,128)(2,1)S(1)}, bf16[4096,256]{1,0:T(8,128)(2,1)}, u32[]{:S(2)}) copy-start(bf16[4096,256]{1,0:T(8,128)(2,1)} %copy-done.3) | copy-start | bytes 6291460
  613.0 5.0 copy-start.11
  613.0 5.3 copy-start.8
  613.0 164.6 %all-to-all-start.3 = ((bf16[2,8,4,2,4,16,256]{6,3,1,5,2,0,4:T(2,128)(2,1)}), bf16[2,8,4,2,4,16,256]{6,3,1,5,2,0,4:T(2,128)(2,1)}, u32[]{:S(2)}, u32[]{:S(2)}) async-start(bf16[2,8,4,2,4,16,256]{6,3,1,5,2,0,4:T(2,128)(2,1)} %copy.178), calls=%async_computation.3 | async-start | bytes 8388608 | tf_op jit(solution)/shard_map/all_to_all | solution.py:186
  617.9 155.9 %all-reduce.3.cloned.1.call-start = ((), (), s32[]{:S(2)}) async-start(), calls=%async_computation.4 | async-start | bytes 2097152 | tf_op jit(solution)/shard_map/psum | solution.py:202
  628.6 3.2 copy-start.9
Sparse Core Ops, SparseCore 0:
  637.5 136.2 all-reduce.2
where the time goes:
time: 807 us; the launch traced here: 794 us
  blocking collectives  194 us (24%)
  waiting for transfers between devices  183 us (23%)
  matrix products  168 us (21%)
  local copies, waits for them, and re-layouts  167 us (21%)
  other arithmetic  55.8 us (7%)
  between operations  14.7 us (2%)
  starting transfers between devices  10.2 us (1%)
    psum x1, waiting for transfers between devices, local(): totals = lax.psum((d_wqkv, d_wout), ('gy', 'gx'))  136 us
    all_to_all x1, blocking collectives, local(): lax.all_to_all(homeward(jnp.stack([mixed_rows, grad_rows]), layout), 'gy'...  97.5 us
    all_to_all x1, blocking collectives, local(): lax.all_to_all(outbound(jnp.stack([tokens, cotangent]), layout), 'gy', sp...  96.7 us
    all_to_all x1, waiting for transfers between devices, local(): lax.all_to_all(lax.all_to_all(outbound(jnp.stack([tokens, cotangent]), la...  46.9 us
    dot_general x1, matrix products, attention_backward(): jnp.einsum('nhmk,nkhd->nmhd', d_scaled, keys, preferred_element_type=jnp....  31 us
    dot_general x1, matrix products, attention_backward(): jnp.einsum('nhmk,nmhd->nkhd', d_scaled, query, preferred_element_type=jnp...  28.6 us
    convert_element_type x2, local copies, waits for them, and re-layouts, attention_backward(): d_qkv = jnp.stack([d_query, d_keys, d_values], axis=2).astype(jnp.bfloat1...  26.5 us
    dot_general x1, matrix products, attention_backward(): jnp.einsum('nmhd,nkhd->nhmk', d_ctx, values, preferred_element_type=jnp.f...  20.4 us
  transfers between devices with their start and end apart: 3, of which 2 were waited for; matrix products, arithmetic and copies ran while one was open for 3% of the time, Pallas kernels for 0%

commit v1 on v0

v1 whole, which is shorter than its diff:
```python
import functools
import math

import jax
import jax.numpy as jnp
from jax import lax
from jax.experimental import pallas as pl
from jax.experimental.pallas import tpu as pltpu
from jax.sharding import PartitionSpec as P

GRID = 8
MEMBERS = GRID * GRID
EPSILON = 1e-05
BATCH = 16
MESH = pl.DeviceIdType.MESH
F32 = jnp.float32
BF16 = jnp.bfloat16


def dot(a, b, da=1, db=0):
    return lax.dot_general(a, b, (((da,), (db,)), ((), ())), preferred_element_type=F32)


def unit_of(wide):
    centre = jnp.mean(wide, axis=-1, keepdims=True)
    shifted = wide - centre
    variance = jnp.mean(shifted * shifted, axis=-1, keepdims=True)
    inverse = lax.rsqrt(variance + EPSILON)
    return shifted * inverse, inverse


def chunk_work(block, result, weights, acc, work, heads):
    gain1, w_qkv, w_out, bias, gain2, w_up, w_down, mask = weights
    wide, xg, gg, normed, qkv, dctx, ctx, dqkv = work
    channels = xg.shape[-1]
    rows = BATCH * MEMBERS
    scale = 1.0 / math.sqrt(channels // heads)
    half = 128

    for tensor, kept in ((0, xg), (1, gg)):
        value = block[tensor].astype(F32).reshape(rows, channels)
        for part in range(channels // half):
            wide[part] = value[:, part * half : (part + 1) * half]
        for group in range(BATCH):
            for part in range(channels // half):
                kept[group * MEMBERS : (group + 1) * MEMBERS, part * half : (part + 1) * half] = wide[
                    part, pl.ds(group, MEMBERS, stride=BATCH), :
                ].astype(BF16)

    step = 256

    def before(index, carry):
        at = pl.ds(pl.multiple_of(index * step, step), step)
        unit, inverse = unit_of(xg[at, :].astype(F32))
        low = (unit * gain1[...]).astype(BF16)
        normed[at, :] = low
        qkv[at, :] = dot(low, w_qkv[...]).astype(BF16)
        dctx[at, :] = dot(gg[at, :], w_out[...], 1, 1).astype(BF16)
        return carry

    lax.fori_loop(0, rows // step, before, 0)

    def one_group(at):
        query = qkv[at, 0:channels]
        keys = qkv[at, channels : 2 * channels]
        values = qkv[at, 2 * channels : 3 * channels]
        spread = mask[...]
        query_wide = jnp.concatenate([query] * heads, axis=0) * spread
        d_wide = jnp.concatenate([dctx[at, :]] * heads, axis=0) * spread
        scores = dot(keys, query_wide, 1, 1) * scale + bias[...]
        top = jnp.max(scores, axis=0, keepdims=True)
        raised = jnp.exp(scores - top)
        probs = raised / jnp.sum(raised, axis=0, keepdims=True)
        low = probs.astype(BF16)
        d_probs = dot(values, d_wide, 1, 1)
        inner = jnp.sum(probs * d_probs, axis=0, keepdims=True)
        d_scaled = (probs * (d_probs - inner) * scale).astype(BF16)

        def gathered(left, right):
            full = dot(left, right, 0, 0)
            lane = lax.broadcasted_iota(jnp.int32, (MEMBERS, channels), 1) // (channels // heads)
            total = full[0:MEMBERS]
            for head in range(1, heads):
                total = jnp.where(lane == head, full[head * MEMBERS : (head + 1) * MEMBERS], total)
            return total

        ctx[at, :] = gathered(low, values).astype(BF16)
        dqkv[at, 0:channels] = gathered(d_scaled, keys).astype(BF16)
        dqkv[at, channels : 2 * channels] = dot(d_scaled, query_wide).astype(BF16)
        dqkv[at, 2 * channels : 3 * channels] = dot(low, d_wide).astype(BF16)

    def attend(index, carry):
        for inner in range(2):
            one_group(pl.ds(pl.multiple_of((2 * index + inner) * MEMBERS, MEMBERS), MEMBERS))
        return carry

    lax.fori_loop(0, BATCH // 2, attend, 0)

    acc[:, 0 : 3 * channels] += dot(normed[...], dqkv[...], 0, 0)
    acc[:, 3 * channels : 4 * channels] += dot(ctx[...], gg[...], 0, 0)

    def spread_out(index, value):
        groups = step // MEMBERS
        for local in range(groups):
            for part in range(channels // half):
                wide[part, pl.ds(index * groups + local, MEMBERS, stride=BATCH), :] = value[
                    local * MEMBERS : (local + 1) * MEMBERS, part * half : (part + 1) * half
                ]

    def finish(tensor):
        value = jnp.concatenate([wide[part] for part in range(channels // half)], axis=1)
        result[tensor] = value.reshape(MEMBERS, BATCH, channels).astype(BF16)

    def forward(index, carry):
        at = pl.ds(pl.multiple_of(index * step, step), step)
        attended = (xg[at, :].astype(F32) + dot(ctx[at, :], w_out[...])).astype(BF16).astype(F32)
        unit, inverse = unit_of(attended)
        low = (unit * gain2[...]).astype(BF16)
        hidden = jax.nn.gelu(dot(low, w_up[...])).astype(BF16)
        spread_out(index, attended + dot(hidden, w_down[...]))
        return carry

    lax.fori_loop(0, rows // step, forward, 0)
    finish(0)

    def backward(index, carry):
        at = pl.ds(pl.multiple_of(index * step, step), step)
        unit, inverse = unit_of(xg[at, :].astype(F32))
        d_unit = dot(dqkv[at, :], w_qkv[...], 1, 1) * gain1[...]
        d_x = inverse * (
            d_unit
            - jnp.mean(d_unit, axis=-1, keepdims=True)
            - unit * jnp.mean(d_unit * unit, axis=-1, keepdims=True)
        )
        spread_out(index, gg[at, :].astype(F32) + d_x)
        return carry

    lax.fori_loop(0, rows // step, backward, 0)
    finish(1)


def kernel(
    plan,
    tokens, cotangent, gain1, w_qkv, w_out, bias, gain2, w_up, w_down, mask,
    mixed, grad_tokens, sums,
    inbox, outbox, acc, wide, xg, gg, normed, qkv, dctx, ctx, dqkv, parts, shares, share, whole,
    sent_in, sent_out, sent_sum, sent_share, chunk_sem, mixed_sem, grad_sem, sum_sem, share_sem,
):
    row_devices, column_devices, row_part, extra, members, splits, strip, per_block, heads = plan
    count = row_devices * column_devices
    gy = lax.axis_index("gy")
    gx = lax.axis_index("gx")
    me = gy * column_devices + gx

    def place(device):
        return device // column_devices, device % column_devices

    def home(device):
        row, column = place(device)
        return row * row_part + column // splits, (column % splits) * strip

    def seat(device):
        row, column = place(device)
        return (row // extra) * GRID + column * members, row % extra

    def peers(body):
        def step(index, carry):
            device = (me + index) % count
            body(index, device, place(device))
            return carry

        lax.fori_loop(1, count, step, 0)

    barrier = pltpu.get_barrier_semaphore()
    peers(lambda index, device, at: pl.semaphore_signal(barrier, inc=1, device_id=at, device_id_type=MESH))
    pl.semaphore_wait(barrier, count - 1)

    my_member, my_extra = seat(me)
    my_row, my_column = home(me)

    def send_block(piece, _):
        chunk = my_extra * per_block + piece
        span = pl.ds(my_member, members)

        def source(device, array):
            row, column = home(device)
            return array.at[row, :, pl.ds(pl.multiple_of(column + piece * BATCH, BATCH), BATCH), :]

        for tensor, array in ((0, tokens), (1, cotangent)):
            pltpu.make_async_copy(
                source(me, array), inbox.at[chunk, tensor, span], chunk_sem.at[chunk]
            ).start()

        def to_peer(index, device, at):
            for tensor, array in ((0, tokens), (1, cotangent)):
                pltpu.make_async_remote_copy(
                    src_ref=source(device, array),
                    dst_ref=inbox.at[chunk, tensor, span],
                    send_sem=sent_in.at[index],
                    recv_sem=chunk_sem.at[chunk],
                    device_id=at,
                    device_id_type=MESH,
                ).start()

        peers(to_peer)
        return _

    lax.fori_loop(0, per_block, send_block, 0)
    acc[...] = jnp.zeros_like(acc)
    weights = (gain1, w_qkv, w_out, bias, gain2, w_up, w_down, mask)
    work = (wide, xg, gg, normed, qkv, dctx, ctx, dqkv)

    def one_chunk(chunk, _):
        pltpu.make_async_copy(inbox.at[chunk], inbox.at[chunk], chunk_sem.at[chunk]).wait()
        chunk_work(inbox.at[chunk], outbox.at[chunk], weights, acc, work, heads)
        part = chunk // per_block
        piece = chunk % per_block
        column = pl.ds(pl.multiple_of(my_column + piece * BATCH, BATCH), BATCH)
        targets = ((0, mixed, mixed_sem), (1, grad_tokens, grad_sem))

        def keep():
            for tensor, array, sem in targets:
                pltpu.make_async_copy(
                    outbox.at[chunk, tensor, pl.ds(my_member, members)], array.at[my_row, :, column, :], sem
                ).start()

        def to_peer(index, device, at):
            member, its = seat(device)

            def send():
                for tensor, array, sem in targets:
                    pltpu.make_async_remote_copy(
                        src_ref=outbox.at[chunk, tensor, pl.ds(member, members)],
                        dst_ref=array.at[my_row, :, column, :],
                        send_sem=sent_out.at[index],
                        recv_sem=sem,
                        device_id=at,
                        device_id_type=MESH,
                    ).start()

            if extra == 1:
                send()
            else:
                pl.when(its == part)(send)

        if extra == 1:
            keep()
        else:
            pl.when(my_extra == part)(keep)
        peers(to_peer)
        return _

    lax.fori_loop(0, extra * per_block, one_chunk, 0)

    height, width = share.shape
    across = acc.shape[1] // width
    for device in range(count):
        top, left = device // across * height, device % across * width
        parts[device] = acc[top : top + height, left : left + width].astype(BF16)
    pltpu.make_async_copy(parts.at[me], shares.at[me], sum_sem).start()
    peers(
        lambda index, device, at: pltpu.make_async_remote_copy(
            src_ref=parts.at[device],
            dst_ref=shares.at[me],
            send_sem=sent_sum.at[index],
            recv_sem=sum_sem,
            device_id=at,
            device_id_type=MESH,
        ).start()
    )
    pltpu.make_async_copy(shares, shares, sum_sem).wait()
    share[...] = jnp.sum(shares[...].astype(F32), axis=0).astype(BF16)
    pltpu.make_async_copy(share, whole.at[me], share_sem).start()
    peers(
        lambda index, device, at: pltpu.make_async_remote_copy(
            src_ref=share,
            dst_ref=whole.at[me],
            send_sem=sent_share.at[index],
            recv_sem=share_sem,
            device_id=at,
            device_id_type=MESH,
        ).start()
    )
    pltpu.make_async_copy(whole, whole, share_sem).wait()
    for device in range(count):
        top, left = device // across * height, device % across * width
        sums[top : top + height, left : left + width] = whole[device].astype(F32)

    def drain(index, device, at):
        moved = inbox.at[pl.ds(0, per_block), :, pl.ds(0, members)]
        pltpu.make_async_copy(moved, moved, sent_in.at[index]).wait()
        pltpu.make_async_copy(moved, moved, sent_out.at[index]).wait()
        pltpu.make_async_copy(share, share, sent_sum.at[index]).wait()
        pltpu.make_async_copy(share, share, sent_share.at[index]).wait()

    peers(drain)
    pltpu.make_async_copy(mixed, mixed, mixed_sem).wait()
    pltpu.make_async_copy(grad_tokens, grad_tokens, grad_sem).wait()


def local(tokens, cotangent, norm1_gain, w_qkv, w_out, pos_bias, norm2_gain, w_up, w_down):
    tile_rows, tile_cols, channels = tokens.shape
    row_devices = lax.axis_size("gy")
    column_devices = lax.axis_size("gx")
    count = row_devices * column_devices
    heads, nodes = pos_bias.shape[:2]
    row_part = tile_rows // row_devices
    extra = row_devices // GRID
    members = GRID // column_devices
    stride = tile_cols // members
    splits = column_devices // row_part
    strip = stride // splits
    per_block = strip // BATCH
    chunks = extra * per_block
    plan = (row_devices, column_devices, row_part, extra, members, splits, strip, per_block, heads)
    factor = 1.0 / math.sqrt(tile_rows * tile_cols * count)
    shape = (tile_rows, members, stride, channels)
    rows = BATCH * MEMBERS
    bias = pos_bias.transpose(2, 0, 1).reshape(nodes, heads * nodes)
    head_of_row = jnp.arange(heads * nodes)[:, None] // nodes
    head_of_lane = jnp.arange(channels)[None, :] // (channels // heads)
    mask = (head_of_row == head_of_lane).astype(BF16)
    width = 4 * channels * channels // (16 * count)
    anywhere = pl.BlockSpec(memory_space=pl.ANY)
    vmem = pl.BlockSpec(memory_space=pltpu.VMEM)
    dma = pltpu.SemaphoreType.DMA
    box = (chunks, 2, MEMBERS, BATCH, channels)
    mixed, grad_tokens, sums = pl.pallas_call(
        functools.partial(kernel, plan),
        out_shape=(
            jax.ShapeDtypeStruct(shape, BF16),
            jax.ShapeDtypeStruct(shape, BF16),
            jax.ShapeDtypeStruct((channels, 4 * channels), F32),
        ),
        in_specs=[anywhere, anywhere] + [vmem] * 8,
        out_specs=(anywhere, anywhere, vmem),
        scratch_shapes=[
            pltpu.VMEM(box, BF16),
            pltpu.VMEM(box, BF16),
            pltpu.VMEM((channels, 4 * channels), F32),
            pltpu.VMEM((channels // 128, rows, 128), F32),
            pltpu.VMEM((rows, channels), BF16),
            pltpu.VMEM((rows, channels), BF16),
            pltpu.VMEM((rows, channels), BF16),
            pltpu.VMEM((rows, 3 * channels), BF16),
            pltpu.VMEM((rows, channels), BF16),
            pltpu.VMEM((rows, channels), BF16),
            pltpu.VMEM((rows, 3 * channels), BF16),
            pltpu.VMEM((count, 16, width), BF16),
            pltpu.VMEM((count, 16, width), BF16),
            pltpu.VMEM((16, width), BF16),
            pltpu.VMEM((count, 16, width), BF16),
            dma((count,)),
            dma((count,)),
            dma((count,)),
            dma((count,)),
            dma((chunks,)),
            dma(()),
            dma(()),
            dma(()),
            dma(()),
        ],
        compiler_params=pltpu.CompilerParams(
            collective_id=0, has_side_effects=True, vmem_limit_bytes=56 * 1024 * 1024
        ),
    )(
        tokens.reshape(shape),
        cotangent.reshape(shape),
        norm1_gain.reshape(1, channels),
        w_qkv,
        w_out,
        bias,
        norm2_gain.reshape(1, channels),
        w_up,
        w_down,
        mask,
    )
    return (
        mixed.reshape(tokens.shape),
        grad_tokens.reshape(tokens.shape),
        sums[:, : 3 * channels] * factor,
        sums[:, 3 * channels :] * factor,
    )


def solution(mesh):
    placed = (P("gy", "gx", None), P("gy", "gx", None), P(), P(), P(), P(), P(), P(), P())
    return jax.shard_map(
        local,
        mesh=mesh,
        in_specs=placed,
        out_specs=(P("gy", "gx", None), P("gy", "gx", None), P(), P()),
        check_vma=False,
    )
```

time: 807 us -> 226 us (0.28); the launches traced: 794 us -> 226 us
  Pallas kernels: 0 us -> 215 us
  blocking collectives: 194 us -> 0 us
  waiting for transfers between devices: 183 us -> 0 us
  matrix products: 168 us -> 0 us
  local copies, waits for them, and re-layouts: 167 us -> 5.39 us
  other arithmetic: 55.8 us -> 4.75 us
  between operations: 14.7 us -> 0.66 us
  starting transfers between devices: 10.2 us -> 0 us
    pallas_call x0 -> x1, Pallas kernels: none -> 215 us  [local(): pl.pallas_call(functools.partial(kernel, plan), out_shape=(jax.ShapeDtype...]
    all_to_all x2 -> x0, blocking collectives: 194 us -> none  [the longest x1 97.5 us: local(): lax.all_to_all(homeward(jnp.stack([mixed_rows, grad_rows]), layout), 'gy'...]
    dot_general x13 -> x0, matrix products: 168 us -> none  [the longest x1 31 us: attention_backward(): jnp.einsum('nhmk,nkhd->nmhd', d_scaled, keys, preferred_element_type=jnp....]
    psum x1 -> x0, waiting for transfers between devices: 136 us -> none  [local(): totals = lax.psum((d_wqkv, d_wout), ('gy', 'gx'))]
    convert_element_type x9 -> x0, local copies, waits for them, and re-layouts: 66.2 us -> none  [the longest x2 26.5 us: attention_backward(): d_qkv = jnp.stack([d_query, d_keys, d_values], axis=2).astype(jnp.bfloat1...]
    all_to_all x2 -> x0, waiting for transfers between devices: 46.9 us -> none  [the longest x1 46.9 us: local(): lax.all_to_all(lax.all_to_all(outbound(jnp.stack([tokens, cotangent]), la...]
    reshape x3 -> x1, local copies, waits for them, and re-layouts: 30.5 us -> 1.72 us  [local(): bias = pos_bias.transpose(2, 0, 1).reshape(nodes, heads * nodes)]
    all_to_all x3 -> x0, local copies, waits for them, and re-layouts: 20.2 us -> none  [the longest x1 8.49 us: local(): lax.all_to_all(outbound(jnp.stack([tokens, cotangent]), layout), 'gy', sp...]
  transfers between devices with their start and end apart: 3 -> 0, of which waited for: 2 -> 0; matrix products, arithmetic and copies ran while one was open for 3% -> 0% of each run, Pallas kernels for 0% -> 0%
where the time goes in v1:
time: 226 us
  Pallas kernels  215 us (95%)
  local copies, waits for them, and re-layouts  5.39 us (2%)
  other arithmetic  4.75 us (2%)
    pallas_call x1, Pallas kernels, local(): pl.pallas_call(functools.partial(kernel, plan), out_shape=(jax.ShapeDtype...  215 us

profile of v1, /device:TPU:25, one launch (start us, length us, event | category | flops | bytes accessed | tf_op | source)
XLA Modules:
  0.0 225.7 jit_solution(13530095019357821014)
XLA Ops:
  0.7 1.7 copy.14.bias
  2.4 0.8 compare_convert_fusion.mask
  3.2 214.9 %shard_map.120 = (bf16[32,2,64,256]{3,2,1,0:T(8,128)(2,1)}, bf16[32,2,64,256]{3,2,1,0:T(8,128)(2,1)}, f32[256,1024]{1,0:T(8,128)}) custom-call(bf16[32,2,64,256]{3,2,1,0:T(8,128)(2,1)} %bitcast.9, bf16[32,2,64,256]{3,2,1,0:T(8,128)(2,1)} %bitcast.10, f32[1,256]{1,0:T(1,128)} %bitcast.14, bf16[256,768]{1,0:T(8,128)(2,1)} %w_qkv.1, bf16[256,256]{1,0:T(8,128)(2,1)} %w_out.1, ...), custom_call_target="tpu_custom_call" | custom-call | tf_op jit(solution)/shard_map/pallas_call | solution.py:328
  218.1 0.0 copy-start.1
  218.1 1.8 slice_multiply_fusion.1
  219.9 2.1 slice_multiply_fusion
  222.0 0.0 copy-done.1
  222.0 0.0 copy-start
  222.0 1.3 copy.17
  223.3 1.0 copy-done
  224.3 1.3 copy.18
  (2 shorter events, 0.0 us)
Async XLA Ops:
  218.1 3.9 %copy-start.1 = (bf16[32,2,64,256]{3,2,1,0:T(8,128)(2,1)S(1)}, bf16[32,2,64,256]{3,2,1,0:T(8,128)(2,1)}, u32[]{:S(2)}) copy-start(bf16[32,2,64,256]{3,2,1,0:T(8,128)(2,1)} %get-tuple-element.7) | copy-start | bytes 6291460
  222.0 2.3 %copy-start = (bf16[32,2,64,256]{3,2,1,0:T(8,128)(2,1)S(1)}, bf16[32,2,64,256]{3,2,1,0:T(8,128)(2,1)}, u32[]{:S(2)}) copy-start(bf16[32,2,64,256]{3,2,1,0:T(8,128)(2,1)} %get-tuple-element.8) | copy-start | bytes 6291460

commit v2 on v1

--- a/solution.py
+++ b/solution.py
@@ -37,17 +37,18 @@
     scale = 1.0 / math.sqrt(channels // heads)
     half = 128
 
-    for tensor, kept in ((0, xg), (1, gg)):
-        value = block[tensor].astype(F32).reshape(rows, channels)
-        for part in range(channels // half):
-            wide[part] = value[:, part * half : (part + 1) * half]
-        for group in range(BATCH):
+    step = 256
+
+    def regroup():
+        for tensor, kept in ((0, xg), (1, gg)):
+            value = block[tensor].astype(F32).reshape(rows, channels)
             for part in range(channels // half):
-                kept[group * MEMBERS : (group + 1) * MEMBERS, part * half : (part + 1) * half] = wide[
-                    part, pl.ds(group, MEMBERS, stride=BATCH), :
-                ].astype(BF16)
-
-    step = 256
+                wide[part] = value[:, part * half : (part + 1) * half]
+            for group in range(BATCH):
+                for part in range(channels // half):
+                    kept[group * MEMBERS : (group + 1) * MEMBERS, part * half : (part + 1) * half] = wide[
+                        part, pl.ds(group, MEMBERS, stride=BATCH), :
+                    ].astype(BF16)
 
     def before(index, carry):
         at = pl.ds(pl.multiple_of(index * step, step), step)
@@ -57,8 +58,6 @@
         qkv[at, :] = dot(low, w_qkv[...]).astype(BF16)
         dctx[at, :] = dot(gg[at, :], w_out[...], 1, 1).astype(BF16)
         return carry
-
-    lax.fori_loop(0, rows // step, before, 0)
 
     def one_group(at):
         query = qkv[at, 0:channels]
@@ -94,10 +93,12 @@
             one_group(pl.ds(pl.multiple_of((2 * index + inner) * MEMBERS, MEMBERS), MEMBERS))
         return carry
 
-    lax.fori_loop(0, BATCH // 2, attend, 0)
-
-    acc[:, 0 : 3 * channels] += dot(normed[...], dqkv[...], 0, 0)
-    acc[:, 3 * channels : 4 * channels] += dot(ctx[...], gg[...], 0, 0)
+    def attention():
+        regroup()
+        lax.fori_loop(0, rows // step, before, 0)
+        lax.fori_loop(0, BATCH // 2, attend, 0)
+        acc[:, 0 : 3 * channels] += dot(normed[...], dqkv[...], 0, 0)
+        acc[:, 3 * channels : 4 * channels] += dot(ctx[...], gg[...], 0, 0)
 
     def spread_out(index, value):
         groups = step // MEMBERS
@@ -119,9 +120,6 @@
         hidden = jax.nn.gelu(dot(low, w_up[...])).astype(BF16)
         spread_out(index, attended + dot(hidden, w_down[...]))
         return carry
-
-    lax.fori_loop(0, rows // step, forward, 0)
-    finish(0)
 
     def backward(index, carry):
         at = pl.ds(pl.multiple_of(index * step, step), step)
@@ -135,18 +133,27 @@
         spread_out(index, gg[at, :].astype(F32) + d_x)
         return carry
 
-    lax.fori_loop(0, rows // step, backward, 0)
-    finish(1)
+    def mlp():
+        lax.fori_loop(0, rows // step, forward, 0)
+        finish(0)
+
+    def token_gradient():
+        lax.fori_loop(0, rows // step, backward, 0)
+        finish(1)
+
+    return attention, mlp, token_gradient
 
 
 def kernel(
     plan,
-    tokens, cotangent, gain1, w_qkv, w_out, bias, gain2, w_up, w_down, mask,
-    mixed, grad_tokens, sums,
-    inbox, outbox, acc, wide, xg, gg, normed, qkv, dctx, ctx, dqkv, parts, shares, share, whole,
-    sent_in, sent_out, sent_sum, sent_share, chunk_sem, mixed_sem, grad_sem, sum_sem, share_sem,
+    tokens, cotangent, gain1, w_qkv, w_out, pos_bias, gain2, w_up, w_down,
+    mixed, grad_tokens, grad_qkv, grad_out,
+    inbox, outbox, acc, wide, xg, gg, normed, qkv, dctx, ctx, dqkv, bias, mask,
+    parts, column_parts, column_sum, row_parts, share, row_shares, shares,
+    sent_in, sent_out, sent_column, sent_row, sent_row_back, sent_column_back,
+    chunk_sem, mixed_sem, grad_sem, sum_sem,
 ):
-    row_devices, column_devices, row_part, extra, members, splits, strip, per_block, heads = plan
+    row_devices, column_devices, row_part, extra, members, splits, strip, per_block, heads, factor = plan
     count = row_devices * column_devices
     gy = lax.axis_index("gy")
     gx = lax.axis_index("gx")
@@ -207,36 +214,39 @@
 
     lax.fori_loop(0, per_block, send_block, 0)
     acc[...] = jnp.zeros_like(acc)
+    bias[...] = pos_bias[...].T
+    channels = mask.shape[1]
+    mask[...] = (
+        lax.broadcasted_iota(jnp.int32, mask.shape, 0) // MEMBERS
+        == lax.broadcasted_iota(jnp.int32, mask.shape, 1) // (channels // heads)
+    ).astype(F32).astype(BF16)
     weights = (gain1, w_qkv, w_out, bias, gain2, w_up, w_down, mask)
     work = (wide, xg, gg, normed, qkv, dctx, ctx, dqkv)
-
-    def one_chunk(chunk, _):
-        pltpu.make_async_copy(inbox.at[chunk], inbox.at[chunk], chunk_sem.at[chunk]).wait()
-        chunk_work(inbox.at[chunk], outbox.at[chunk], weights, acc, work, heads)
+    targets = ((mixed, mixed_sem), (grad_tokens, grad_sem))
+
+    def send_home(chunk, tensor):
         part = chunk // per_block
         piece = chunk % per_block
         column = pl.ds(pl.multiple_of(my_column + piece * BATCH, BATCH), BATCH)
-        targets = ((0, mixed, mixed_sem), (1, grad_tokens, grad_sem))
+        array, sem = targets[tensor]
 
         def keep():
-            for tensor, array, sem in targets:
-                pltpu.make_async_copy(
-                    outbox.at[chunk, tensor, pl.ds(my_member, members)], array.at[my_row, :, column, :], sem
-                ).start()
+            pltpu.make_async_copy(
+                outbox.at[chunk, tensor, pl.ds(my_member, members)], array.at[my_row, :, column, :], sem
+            ).start()
 
         def to_peer(index, device, at):
             member, its = seat(device)
 
             def send():
-                for tensor, array, sem in targets:
-                    pltpu.make_async_remote_copy(
-                        src_ref=outbox.at[chunk, tensor, pl.ds(member, members)],
-                        dst_ref=array.at[my_row, :, column, :],
-                        send_sem=sent_out.at[index],
-                        recv_sem=sem,
-                        device_id=at,
-                        device_id_type=MESH,
-                    ).start()
+                pltpu.make_async_remote_copy(
+                    src_ref=outbox.at[chunk, tensor, pl.ds(member, members)],
+                    dst_ref=array.at[my_row, :, column, :],
+                    send_sem=sent_out.at[index],
+                    recv_sem=sem,
+                    device_id=at,
+                    device_id_type=MESH,
+                ).start()
 
             if extra == 1:
                 send()
@@ -248,52 +258,99 @@
         else:
             pl.when(my_extra == part)(keep)
         peers(to_peer)
-        return _
-
-    lax.fori_loop(0, extra * per_block, one_chunk, 0)
+
+    def exchange(stage, axis, source, target, sent):
+        size, own = ((row_devices, gy), (column_devices, gx))[axis]
+        pltpu.make_async_copy(source(own), target.at[own], sum_sem.at[stage]).start()
+
+        def step(index, carry):
+            other = (own + index) % size
+            pltpu.make_async_remote_copy(
+                src_ref=source(other),
+                dst_ref=target.at[own],
+                send_sem=sent.at[index],
+                recv_sem=sum_sem.at[stage],
+                device_id=((other, gx), (gy, other))[axis],
+                device_id_type=MESH,
+            ).start()
+            return carry
+
+        lax.fori_loop(1, size, step, 0)
+
+    def arrive(stage, target):
+        pltpu.make_async_copy(target, target, sum_sem.at[stage]).wait()
 
     height, width = share.shape
     across = acc.shape[1] // width
-    for device in range(count):
-        top, left = device // across * height, device % across * width
-        parts[device] = acc[top : top + height, left : left + width].astype(BF16)
-    pltpu.make_async_copy(parts.at[me], shares.at[me], sum_sem).start()
-    peers(
-        lambda index, device, at: pltpu.make_async_remote_copy(
-            src_ref=parts.at[device],
-            dst_ref=shares.at[me],
-            send_sem=sent_sum.at[index],
-            recv_sem=sum_sem,
-            device_id=at,
-            device_id_type=MESH,
-        ).start()
-    )
-    pltpu.make_async_copy(shares, shares, sum_sem).wait()
-    share[...] = jnp.sum(shares[...].astype(F32), axis=0).astype(BF16)
-    pltpu.make_async_copy(share, whole.at[me], share_sem).start()
-    peers(
-        lambda index, device, at: pltpu.make_async_remote_copy(
-            src_ref=share,
-            dst_ref=whole.at[me],
-            send_sem=sent_share.at[index],
-            recv_sem=share_sem,
-            device_id=at,
-            device_id_type=MESH,
-        ).start()
-    )
-    pltpu.make_async_copy(whole, whole, share_sem).wait()
-    for device in range(count):
-        top, left = device // across * height, device % across * width
-        sums[top : top + height, left : left + width] = whole[device].astype(F32)
+
+    def areas():
+        for place_of in range(count):
+            yield (
+                place_of // row_devices,
+                place_of % row_devices,
+                place_of // across * height,
+                place_of % across * width,
+            )
+
+    chunks = extra * per_block
+
+    def one_chunk(chunk, _):
+        pltpu.make_async_copy(inbox.at[chunk], inbox.at[chunk], chunk_sem.at[chunk]).wait()
+        attention, mlp, token_gradient = chunk_work(
+            inbox.at[chunk], outbox.at[chunk], weights, acc, work, heads
+        )
+        attention()
+
+        @pl.when(chunk == chunks - 1)
+        def begin_sums():
+            for column, row, top, left in areas():
+                parts[column, row] = acc[top : top + height, left : left + width].astype(BF16)
+            exchange(0, 1, lambda other: parts.at[other], column_parts, sent_column)
+            send_home(chunks - 2, 0)
+
+        mlp()
+        pl.when(chunk < chunks - 2)(lambda: send_home(chunk, 0))
+        token_gradient()
+        pl.when(chunk < chunks - 2)(lambda: send_home(chunk, 1))
+        return _
+
+    lax.fori_loop(0, chunks, one_chunk, 0)
+
+    arrive(0, column_parts)
+    column_sum[...] = jnp.sum(column_parts[...].astype(F32), axis=0).astype(BF16)
+    exchange(1, 0, lambda other: column_sum.at[other], row_parts, sent_row)
+    send_home(chunks - 2, 1)
+    arrive(1, row_parts)
+    share[...] = jnp.sum(row_parts[...].astype(F32), axis=0).astype(BF16)
+    exchange(2, 0, lambda other: share, row_shares, sent_row_back)
+    send_home(chunks - 1, 0)
+    arrive(2, row_shares)
+    exchange(3, 1, lambda other: row_shares, shares, sent_column_back)
+    send_home(chunks - 1, 1)
+    arrive(3, shares)
+    for column, row, top, left in areas():
+        value = shares[column, row].astype(F32) * factor
+        cut = min(max(3 * channels - left, 0), width)
+        if cut > 0:
+            grad_qkv[top : top + height, left : left + cut] = value[:, :cut]
+        if cut < width:
+            start = left + cut - 3 * channels
+            grad_out[top : top + height, start : start + width - cut] = value[:, cut:]
 
     def drain(index, device, at):
         moved = inbox.at[pl.ds(0, per_block), :, pl.ds(0, members)]
         pltpu.make_async_copy(moved, moved, sent_in.at[index]).wait()
         pltpu.make_async_copy(moved, moved, sent_out.at[index]).wait()
-        pltpu.make_async_copy(share, share, sent_sum.at[index]).wait()
-        pltpu.make_async_copy(share, share, sent_share.at[index]).wait()
 
     peers(drain)
+    for sent, size, moved in (
+        (sent_column, column_devices, row_parts),
+        (sent_row, row_devices, share),
+        (sent_row_back, row_devices, share),
+        (sent_column_back, column_devices, row_parts),
+    ):
+        for index in range(1, size):
+            pltpu.make_async_copy(moved, moved, sent.at[index]).wait()
     pltpu.make_async_copy(mixed, mixed, mixed_sem).wait()
     pltpu.make_async_copy(grad_tokens, grad_tokens, grad_sem).wait()
 
@@ -312,28 +369,25 @@
     strip = stride // splits
     per_block = strip // BATCH
     chunks = extra * per_block
-    plan = (row_devices, column_devices, row_part, extra, members, splits, strip, per_block, heads)
     factor = 1.0 / math.sqrt(tile_rows * tile_cols * count)
+    plan = (row_devices, column_devices, row_part, extra, members, splits, strip, per_block, heads, factor)
     shape = (tile_rows, members, stride, channels)
     rows = BATCH * MEMBERS
-    bias = pos_bias.transpose(2, 0, 1).reshape(nodes, heads * nodes)
-    head_of_row = jnp.arange(heads * nodes)[:, None] // nodes
-    head_of_lane = jnp.arange(channels)[None, :] // (channels // heads)
-    mask = (head_of_row == head_of_lane).astype(BF16)
     width = 4 * channels * channels // (16 * count)
     anywhere = pl.BlockSpec(memory_space=pl.ANY)
     vmem = pl.BlockSpec(memory_space=pltpu.VMEM)
     dma = pltpu.SemaphoreType.DMA
     box = (chunks, 2, MEMBERS, BATCH, channels)
-    mixed, grad_tokens, sums = pl.pallas_call(
+    mixed, grad_tokens, grad_qkv, grad_out = pl.pallas_call(
         functools.partial(kernel, plan),
         out_shape=(
             jax.ShapeDtypeStruct(shape, BF16),
             jax.ShapeDtypeStruct(shape, BF16),
-            jax.ShapeDtypeStruct((channels, 4 * channels), F32),
+            jax.ShapeDtypeStruct((channels, 3 * channels), F32),
+            jax.ShapeDtypeStruct((channels, channels), F32),
         ),
-        in_specs=[anywhere, anywhere] + [vmem] * 8,
-        out_specs=(anywhere, anywhere, vmem),
+        in_specs=[anywhere, anywhere] + [vmem] * 7,
+        out_specs=(anywhere, anywhere, vmem, vmem),
         scratch_shapes=[
             pltpu.VMEM(box, BF16),
             pltpu.VMEM(box, BF16),
@@ -346,19 +400,25 @@
             pltpu.VMEM((rows, channels), BF16),
             pltpu.VMEM((rows, channels), BF16),
             pltpu.VMEM((rows, 3 * channels), BF16),
-            pltpu.VMEM((count, 16, width), BF16),
-            pltpu.VMEM((count, 16, width), BF16),
+            pltpu.VMEM((nodes, heads * nodes), F32),
+            pltpu.VMEM((heads * nodes, channels), BF16),
+            pltpu.VMEM((column_devices, row_devices, 16, width), BF16),
+            pltpu.VMEM((column_devices, row_devices, 16, width), BF16),
+            pltpu.VMEM((row_devices, 16, width), BF16),
+            pltpu.VMEM((row_devices, 16, width), BF16),
             pltpu.VMEM((16, width), BF16),
-            pltpu.VMEM((count, 16, width), BF16),
+            pltpu.VMEM((row_devices, 16, width), BF16),
+            pltpu.VMEM((column_devices, row_devices, 16, width), BF16),
             dma((count,)),
             dma((count,)),
-            dma((count,)),
-            dma((count,)),
+            dma((column_devices,)),
+            dma((row_devices,)),
+            dma((row_devices,)),
+            dma((column_devices,)),
             dma((chunks,)),
             dma(()),
             dma(()),
-            dma(()),
-            dma(()),
+            dma((4,)),
         ],
         compiler_params=pltpu.CompilerParams(
             collective_id=0, has_side_effects=True, vmem_limit_bytes=56 * 1024 * 1024
@@ -369,17 +429,16 @@
         norm1_gain.reshape(1, channels),
         w_qkv,
         w_out,
-        bias,
+        pos_bias.reshape(heads * nodes, nodes),
         norm2_gain.reshape(1, channels),
         w_up,
         w_down,
-        mask,
     )
     return (
         mixed.reshape(tokens.shape),
         grad_tokens.reshape(tokens.shape),
-        sums[:, : 3 * channels] * factor,
-        sums[:, 3 * channels :] * factor,
+        grad_qkv,
+        grad_out,
     )
 
 

time: 226 us -> 203 us (0.90)
  Pallas kernels: 215 us -> 194 us
  other arithmetic: 4.75 us -> 0 us
    pallas_call x1, Pallas kernels: 215 us -> 194 us  [local(): pl.pallas_call(functools.partial(kernel, plan), out_shape=(jax.ShapeDtype...]
    mul x2 -> x0, other arithmetic: 3.91 us -> none  [the longest x1 2.08 us: local(): sums[:, :3 * channels] * factor]
    unnamed x6 -> x10, local copies, waits for them, and re-layouts: 3.67 us -> 6.54 us
where the time goes in v2:
time: 203 us; the launch traced here: 202 us
  Pallas kernels  194 us (96%)
  local copies, waits for them, and re-layouts  6.54 us (3%)
    pallas_call x1, Pallas kernels, local(): pl.pallas_call(functools.partial(kernel, plan), out_shape=(jax.ShapeDtype...  194 us
    unnamed x10, local copies, waits for them, and re-layouts  6.54 us

profile of v2, /device:TPU:25, one launch (start us, length us, event | category | flops | bytes accessed | tf_op | source)
XLA Modules:
  0.0 201.6 jit_solution(12391099947713778865)
XLA Ops:
  0.6 194.4 %shard_map.120 = (bf16[32,2,64,256]{3,2,1,0:T(8,128)(2,1)}, bf16[32,2,64,256]{3,2,1,0:T(8,128)(2,1)}, f32[256,768]{1,0:T(8,128)}, f32[256,256]{1,0:T(8,128)}) custom-call(bf16[32,2,64,256]{3,2,1,0:T(8,128)(2,1)} %bitcast.7, bf16[32,2,64,256]{3,2,1,0:T(8,128)(2,1)} %bitcast.8, f32[1,256]{1,0:T(1,128)} %bitcast.12, bf16[256,768]{1,0:T(8,128)(2,1)} %w_qkv.1, ...), custom_call_target="tpu_custom_call" | custom-call | tf_op jit(solution)/shard_map/pallas_call | solution.py:381
  195.0 0.0 copy-start
  195.0 3.3 %copy.17 = bf16[32,128,256]{2,1,0:T(8,128)(2,1)} copy(bf16[32,128,256]{2,1,0:T(8,128)(2,1)} %bitcast.10) | data formatting | bytes 4194304
  198.3 0.0 copy-done
  198.3 0.0 copy-start.1
  198.3 0.0 copy-start.2
  198.3 1.3 copy.18
  199.6 0.4 copy-done.1
  200.0 0.9 copy.19
  200.9 0.0 copy-done.2
  200.9 0.7 copy.20
Async XLA Ops:
  195.0 3.3 %copy-start = (bf16[32,2,64,256]{3,2,1,0:T(8,128)(2,1)S(1)}, bf16[32,2,64,256]{3,2,1,0:T(8,128)(2,1)}, u32[]{:S(2)}) copy-start(bf16[32,2,64,256]{3,2,1,0:T(8,128)(2,1)} %get-tuple-element.9) | copy-start | bytes 6291460
  198.3 1.7 copy-start.1
  198.3 2.6 %copy-start.2 = (f32[256,256]{1,0:T(8,128)S(1)}, f32[256,256]{1,0:T(8,128)}, u32[]{:S(2)}) copy-start(f32[256,256]{1,0:T(8,128)} %get-tuple-element.19) | copy-start | bytes 786436

commit v3 on v2

--- a/solution.py
+++ b/solution.py
@@ -12,6 +12,7 @@
 MEMBERS = GRID * GRID
 EPSILON = 1e-05
 BATCH = 16
+STRIDE = 13
 MESH = pl.DeviceIdType.MESH
 F32 = jnp.float32
 BF16 = jnp.bfloat16
@@ -172,7 +173,7 @@
 
     def peers(body):
         def step(index, carry):
-            device = (me + index) % count
+            device = (me + index * STRIDE) % count
             body(index, device, place(device))
             return carry
 

time: 203 us -> 204 us (level)
  no operation moved by 1% of the time
where the time goes in v3:
time: 204 us; the launch traced here: 202 us
  Pallas kernels  195 us (96%)
  local copies, waits for them, and re-layouts  6.54 us (3%)
    pallas_call x1, Pallas kernels, local(): pl.pallas_call(functools.partial(kernel, plan), out_shape=(jax.ShapeDtype...  195 us
    unnamed x10, local copies, waits for them, and re-layouts  6.54 us

profile of v3, /device:TPU:25, one launch (start us, length us, event | category | flops | bytes accessed | tf_op | source)
XLA Modules:
  0.0 202.3 jit_solution(3996123866997814015)
XLA Ops:
  0.6 195.1 %shard_map.120 = (bf16[32,2,64,256]{3,2,1,0:T(8,128)(2,1)}, bf16[32,2,64,256]{3,2,1,0:T(8,128)(2,1)}, f32[256,768]{1,0:T(8,128)}, f32[256,256]{1,0:T(8,128)}) custom-call(bf16[32,2,64,256]{3,2,1,0:T(8,128)(2,1)} %bitcast.7, bf16[32,2,64,256]{3,2,1,0:T(8,128)(2,1)} %bitcast.8, f32[1,256]{1,0:T(1,128)} %bitcast.12, bf16[256,768]{1,0:T(8,128)(2,1)} %w_qkv.1, ...), custom_call_target="tpu_custom_call" | custom-call | tf_op jit(solution)/shard_map/pallas_call | solution.py:382
  195.7 0.0 copy-start
  195.7 3.3 %copy.17 = bf16[32,128,256]{2,1,0:T(8,128)(2,1)} copy(bf16[32,128,256]{2,1,0:T(8,128)(2,1)} %bitcast.10) | data formatting | bytes 4194304
  199.0 0.0 copy-done
  199.0 0.0 copy-start.1
  199.0 0.0 copy-start.2
  199.0 1.3 copy.18
  200.4 0.4 copy-done.1
  200.7 0.9 copy.19
  201.6 0.0 copy-done.2
  201.6 0.7 copy.20
Async XLA Ops:
  195.7 3.3 %copy-start = (bf16[32,2,64,256]{3,2,1,0:T(8,128)(2,1)S(1)}, bf16[32,2,64,256]{3,2,1,0:T(8,128)(2,1)}, u32[]{:S(2)}) copy-start(bf16[32,2,64,256]{3,2,1,0:T(8,128)(2,1)} %get-tuple-element.9) | copy-start | bytes 6291460
  199.0 1.7 copy-start.1
  199.0 2.6 %copy-start.2 = (f32[256,256]{1,0:T(8,128)S(1)}, f32[256,256]{1,0:T(8,128)}, u32[]{:S(2)}) copy-start(f32[256,256]{1,0:T(8,128)} %get-tuple-element.19) | copy-start | bytes 786436

commit v4 on v2

--- a/solution.py
+++ b/solution.py
@@ -59,14 +59,20 @@
         dctx[at, :] = dot(gg[at, :], w_out[...], 1, 1).astype(BF16)
         return carry
 
-    def one_group(at):
-        query = qkv[at, 0:channels]
-        keys = qkv[at, channels : 2 * channels]
-        values = qkv[at, 2 * channels : 3 * channels]
+    lanes = 128
+    head_width = channels // heads
+    span_heads = lanes // head_width
+    span = span_heads * MEMBERS
+
+    def some_heads(at, which):
+        first = which * lanes
+        query = qkv[at, first : first + lanes]
+        keys = qkv[at, channels + first : channels + first + lanes]
+        values = qkv[at, 2 * channels + first : 2 * channels + first + lanes]
         spread = mask[...]
-        query_wide = jnp.concatenate([query] * heads, axis=0) * spread
-        d_wide = jnp.concatenate([dctx[at, :]] * heads, axis=0) * spread
-        scores = dot(keys, query_wide, 1, 1) * scale + bias[...]
+        query_wide = jnp.concatenate([query] * span_heads, axis=0) * spread
+        d_wide = jnp.concatenate([dctx[at, first : first + lanes]] * span_heads, axis=0) * spread
+        scores = dot(keys, query_wide, 1, 1) * scale + bias[:, which * span : (which + 1) * span]
         top = jnp.max(scores, axis=0, keepdims=True)
         raised = jnp.exp(scores - top)
         probs = raised / jnp.sum(raised, axis=0, keepdims=True)
@@ -77,26 +83,30 @@
 
         def gathered(left, right):
             full = dot(left, right, 0, 0)
-            lane = lax.broadcasted_iota(jnp.int32, (MEMBERS, channels), 1) // (channels // heads)
+            lane = lax.broadcasted_iota(jnp.int32, (MEMBERS, lanes), 1) // head_width
             total = full[0:MEMBERS]
-            for head in range(1, heads):
+            for head in range(1, span_heads):
                 total = jnp.where(lane == head, full[head * MEMBERS : (head + 1) * MEMBERS], total)
             return total
 
-        ctx[at, :] = gathered(low, values).astype(BF16)
-        dqkv[at, 0:channels] = gathered(d_scaled, keys).astype(BF16)
-        dqkv[at, channels : 2 * channels] = dot(d_scaled, query_wide).astype(BF16)
-        dqkv[at, 2 * channels : 3 * channels] = dot(low, d_wide).astype(BF16)
+        ctx[at, first : first + lanes] = gathered(low, values).astype(BF16)
+        dqkv[at, first : first + lanes] = gathered(d_scaled, keys).astype(BF16)
+        dqkv[at, channels + first : channels + first + lanes] = dot(d_scaled, query_wide).astype(BF16)
+        dqkv[at, 2 * channels + first : 2 * channels + first + lanes] = dot(low, d_wide).astype(BF16)
+
+    together = 4
 
     def attend(index, carry):
-        for inner in range(2):
-            one_group(pl.ds(pl.multiple_of((2 * index + inner) * MEMBERS, MEMBERS), MEMBERS))
+        for inner in range(together):
+            at = pl.ds(pl.multiple_of((together * index + inner) * MEMBERS, MEMBERS), MEMBERS)
+            for which in range(channels // lanes):
+                some_heads(at, which)
         return carry
 
     def attention():
         regroup()
         lax.fori_loop(0, rows // step, before, 0)
-        lax.fori_loop(0, BATCH // 2, attend, 0)
+        lax.fori_loop(0, BATCH // together, attend, 0)
         acc[:, 0 : 3 * channels] += dot(normed[...], dqkv[...], 0, 0)
         acc[:, 3 * channels : 4 * channels] += dot(ctx[...], gg[...], 0, 0)
 
@@ -215,7 +225,7 @@
     lax.fori_loop(0, per_block, send_block, 0)
     acc[...] = jnp.zeros_like(acc)
     bias[...] = pos_bias[...].T
-    channels = mask.shape[1]
+    channels = acc.shape[0]
     mask[...] = (
         lax.broadcasted_iota(jnp.int32, mask.shape, 0) // MEMBERS
         == lax.broadcasted_iota(jnp.int32, mask.shape, 1) // (channels // heads)
@@ -306,10 +316,10 @@
             for column, row, top, left in areas():
                 parts[column, row] = acc[top : top + height, left : left + width].astype(BF16)
             exchange(0, 1, lambda other: parts.at[other], column_parts, sent_column)
-            send_home(chunks - 2, 0)
+            send_home(chunks - 2, 1)
 
         mlp()
-        pl.when(chunk < chunks - 2)(lambda: send_home(chunk, 0))
+        send_home(chunk, 0)
         token_gradient()
         pl.when(chunk < chunks - 2)(lambda: send_home(chunk, 1))
         return _
@@ -319,14 +329,12 @@
     arrive(0, column_parts)
     column_sum[...] = jnp.sum(column_parts[...].astype(F32), axis=0).astype(BF16)
     exchange(1, 0, lambda other: column_sum.at[other], row_parts, sent_row)
-    send_home(chunks - 2, 1)
     arrive(1, row_parts)
     share[...] = jnp.sum(row_parts[...].astype(F32), axis=0).astype(BF16)
     exchange(2, 0, lambda other: share, row_shares, sent_row_back)
-    send_home(chunks - 1, 0)
+    send_home(chunks - 1, 1)
     arrive(2, row_shares)
     exchange(3, 1, lambda other: row_shares, shares, sent_column_back)
-    send_home(chunks - 1, 1)
     arrive(3, shares)
     for column, row, top, left in areas():
         value = shares[column, row].astype(F32) * factor
@@ -401,7 +409,7 @@
             pltpu.VMEM((rows, channels), BF16),
             pltpu.VMEM((rows, 3 * channels), BF16),
             pltpu.VMEM((nodes, heads * nodes), F32),
-            pltpu.VMEM((heads * nodes, channels), BF16),
+            pltpu.VMEM((128 * heads // channels * nodes, 128), BF16),
             pltpu.VMEM((column_devices, row_devices, 16, width), BF16),
             pltpu.VMEM((column_devices, row_devices, 16, width), BF16),
             pltpu.VMEM((row_devices, 16, width), BF16),

time: 203 us -> 206 us (1.015)
  no operation moved by 1% of the time
where the time goes in v4:
time: 206 us; the launch traced here: 203 us
  Pallas kernels  196 us (95%)
  local copies, waits for them, and re-layouts  6.54 us (3%)
    pallas_call x1, Pallas kernels, local(): pl.pallas_call(functools.partial(kernel, plan), out_shape=(jax.ShapeDtype...  196 us
    unnamed x10, local copies, waits for them, and re-layouts  6.54 us

profile of v4, /device:TPU:25, one launch (start us, length us, event | category | flops | bytes accessed | tf_op | source)
XLA Modules:
  0.0 203.0 jit_solution(14212956937665380051)
XLA Ops:
  0.6 195.8 %shard_map.120 = (bf16[32,2,64,256]{3,2,1,0:T(8,128)(2,1)}, bf16[32,2,64,256]{3,2,1,0:T(8,128)(2,1)}, f32[256,768]{1,0:T(8,128)}, f32[256,256]{1,0:T(8,128)}) custom-call(bf16[32,2,64,256]{3,2,1,0:T(8,128)(2,1)} %bitcast.7, bf16[32,2,64,256]{3,2,1,0:T(8,128)(2,1)} %bitcast.8, f32[1,256]{1,0:T(1,128)} %bitcast.12, bf16[256,768]{1,0:T(8,128)(2,1)} %w_qkv.1, ...), custom_call_target="tpu_custom_call" | custom-call | tf_op jit(solution)/shard_map/pallas_call | solution.py:389
  196.4 0.0 copy-start
  196.4 3.3 %copy.17 = bf16[32,128,256]{2,1,0:T(8,128)(2,1)} copy(bf16[32,128,256]{2,1,0:T(8,128)(2,1)} %bitcast.10) | data formatting | bytes 4194304
  199.7 0.0 copy-done
  199.7 0.0 copy-start.1
  199.7 0.0 copy-start.2
  199.7 1.3 copy.18
  201.0 0.4 copy-done.1
  201.4 0.9 copy.19
  202.3 0.0 copy-done.2
  202.3 0.7 copy.20
Async XLA Ops:
  196.4 3.3 %copy-start = (bf16[32,2,64,256]{3,2,1,0:T(8,128)(2,1)S(1)}, bf16[32,2,64,256]{3,2,1,0:T(8,128)(2,1)}, u32[]{:S(2)}) copy-start(bf16[32,2,64,256]{3,2,1,0:T(8,128)(2,1)} %get-tuple-element.9) | copy-start | bytes 6291460
  199.7 1.7 copy-start.1
  199.7 2.6 %copy-start.2 = (f32[256,256]{1,0:T(8,128)S(1)}, f32[256,256]{1,0:T(8,128)}, u32[]{:S(2)}) copy-start(f32[256,256]{1,0:T(8,128)} %get-tuple-element.19) | copy-start | bytes 786436

commit v5 on v4

--- a/solution.py
+++ b/solution.py
@@ -12,6 +12,7 @@
 MEMBERS = GRID * GRID
 EPSILON = 1e-05
 BATCH = 16
+PIECE = 2 * BATCH
 MESH = pl.DeviceIdType.MESH
 F32 = jnp.float32
 BF16 = jnp.bfloat16
@@ -157,11 +158,11 @@
 def kernel(
     plan,
     tokens, cotangent, gain1, w_qkv, w_out, pos_bias, gain2, w_up, w_down,
-    mixed, grad_tokens, grad_qkv, grad_out,
+    results, grad_qkv, grad_out,
     inbox, outbox, acc, wide, xg, gg, normed, qkv, dctx, ctx, dqkv, bias, mask,
     parts, column_parts, column_sum, row_parts, share, row_shares, shares,
     sent_in, sent_out, sent_column, sent_row, sent_row_back, sent_column_back,
-    chunk_sem, mixed_sem, grad_sem, sum_sem,
+    chunk_sem, home_sem, sum_sem,
 ):
     row_devices, column_devices, row_part, extra, members, splits, strip, per_block, heads, factor = plan
     count = row_devices * column_devices
@@ -195,26 +196,28 @@
     my_member, my_extra = seat(me)
     my_row, my_column = home(me)
 
+    pieces = strip // PIECE
+
     def send_block(piece, _):
-        chunk = my_extra * per_block + piece
+        part = my_extra * pieces + piece
         span = pl.ds(my_member, members)
 
         def source(device, array):
             row, column = home(device)
-            return array.at[row, :, pl.ds(pl.multiple_of(column + piece * BATCH, BATCH), BATCH), :]
+            return array.at[row, :, pl.ds(pl.multiple_of(column + piece * PIECE, PIECE), PIECE), :]
 
         for tensor, array in ((0, tokens), (1, cotangent)):
             pltpu.make_async_copy(
-                source(me, array), inbox.at[chunk, tensor, span], chunk_sem.at[chunk]
+                source(me, array), inbox.at[part, tensor, span], chunk_sem.at[part]
             ).start()
 
         def to_peer(index, device, at):
             for tensor, array in ((0, tokens), (1, cotangent)):
                 pltpu.make_async_remote_copy(
                     src_ref=source(device, array),
-                    dst_ref=inbox.at[chunk, tensor, span],
+                    dst_ref=inbox.at[part, tensor, span],
                     send_sem=sent_in.at[index],
-                    recv_sem=chunk_sem.at[chunk],
+                    recv_sem=chunk_sem.at[part],
                     device_id=at,
                     device_id_type=MESH,
                 ).start()
@@ -222,7 +225,7 @@
         peers(to_peer)
         return _
 
-    lax.fori_loop(0, per_block, send_block, 0)
+    lax.fori_loop(0, pieces, send_block, 0)
     acc[...] = jnp.zeros_like(acc)
     bias[...] = pos_bias[...].T
     channels = acc.shape[0]
@@ -232,17 +235,15 @@
     ).astype(F32).astype(BF16)
     weights = (gain1, w_qkv, w_out, bias, gain2, w_up, w_down, mask)
     work = (wide, xg, gg, normed, qkv, dctx, ctx, dqkv)
-    targets = ((mixed, mixed_sem), (grad_tokens, grad_sem))
-
-    def send_home(chunk, tensor):
+
+    def send_home(chunk):
         part = chunk // per_block
         piece = chunk % per_block
         column = pl.ds(pl.multiple_of(my_column + piece * BATCH, BATCH), BATCH)
-        array, sem = targets[tensor]
 
         def keep():
             pltpu.make_async_copy(
-                outbox.at[chunk, tensor, pl.ds(my_member, members)], array.at[my_row, :, column, :], sem
+                outbox.at[chunk, :, pl.ds(my_member, members)], results.at[:, my_row, :, column, :], home_sem
             ).start()
 
         def to_peer(index, device, at):
@@ -250,10 +251,10 @@
 
             def send():
                 pltpu.make_async_remote_copy(
-                    src_ref=outbox.at[chunk, tensor, pl.ds(member, members)],
-                    dst_ref=array.at[my_row, :, column, :],
+                    src_ref=outbox.at[chunk, :, pl.ds(member, members)],
+                    dst_ref=results.at[:, my_row, :, column, :],
                     send_sem=sent_out.at[index],
-                    recv_sem=sem,
+                    recv_sem=home_sem,
                     device_id=at,
                     device_id_type=MESH,
                 ).start()
@@ -304,10 +305,18 @@
 
     chunks = extra * per_block
 
+    halves = PIECE // BATCH
+
     def one_chunk(chunk, _):
-        pltpu.make_async_copy(inbox.at[chunk], inbox.at[chunk], chunk_sem.at[chunk]).wait()
+        part = chunk // halves
+        at = pl.ds(pl.multiple_of(chunk % halves * BATCH, BATCH), BATCH)
+
+        @pl.when(chunk % halves == 0)
+        def piece_here():
+            pltpu.make_async_copy(inbox.at[part], inbox.at[part], chunk_sem.at[part]).wait()
+
         attention, mlp, token_gradient = chunk_work(
-            inbox.at[chunk], outbox.at[chunk], weights, acc, work, heads
+            inbox.at[part, :, :, at, :], outbox.at[chunk], weights, acc, work, heads
         )
         attention()
 
@@ -316,12 +325,10 @@
             for column, row, top, left in areas():
                 parts[column, row] = acc[top : top + height, left : left + width].astype(BF16)
             exchange(0, 1, lambda other: parts.at[other], column_parts, sent_column)
-            send_home(chunks - 2, 1)
 
         mlp()
-        send_home(chunk, 0)
         token_gradient()
-        pl.when(chunk < chunks - 2)(lambda: send_home(chunk, 1))
+        pl.when(chunk < chunks - 2)(lambda: send_home(chunk))
         return _
 
     lax.fori_loop(0, chunks, one_chunk, 0)
@@ -329,10 +336,11 @@
     arrive(0, column_parts)
     column_sum[...] = jnp.sum(column_parts[...].astype(F32), axis=0).astype(BF16)
     exchange(1, 0, lambda other: column_sum.at[other], row_parts, sent_row)
+    send_home(chunks - 2)
     arrive(1, row_parts)
     share[...] = jnp.sum(row_parts[...].astype(F32), axis=0).astype(BF16)
     exchange(2, 0, lambda other: share, row_shares, sent_row_back)
-    send_home(chunks - 1, 1)
+    send_home(chunks - 1)
     arrive(2, row_shares)
     exchange(3, 1, lambda other: row_shares, shares, sent_column_back)
     arrive(3, shares)
@@ -346,7 +354,7 @@
             grad_out[top : top + height, start : start + width - cut] = value[:, cut:]
 
     def drain(index, device, at):
-        moved = inbox.at[pl.ds(0, per_block), :, pl.ds(0, members)]
+        moved = outbox.at[pl.ds(0, per_block), :, pl.ds(0, members)]
         pltpu.make_async_copy(moved, moved, sent_in.at[index]).wait()
         pltpu.make_async_copy(moved, moved, sent_out.at[index]).wait()
 
@@ -359,8 +367,7 @@
     ):
         for index in range(1, size):
             pltpu.make_async_copy(moved, moved, sent.at[index]).wait()
-    pltpu.make_async_copy(mixed, mixed, mixed_sem).wait()
-    pltpu.make_async_copy(grad_tokens, grad_tokens, grad_sem).wait()
+    pltpu.make_async_copy(results, results, home_sem).wait()
 
 
 def local(tokens, cotangent, norm1_gain, w_qkv, w_out, pos_bias, norm2_gain, w_up, w_down):
@@ -385,20 +392,20 @@
     anywhere = pl.BlockSpec(memory_space=pl.ANY)
     vmem = pl.BlockSpec(memory_space=pltpu.VMEM)
     dma = pltpu.SemaphoreType.DMA
-    box = (chunks, 2, MEMBERS, BATCH, channels)
-    mixed, grad_tokens, grad_qkv, grad_out = pl.pallas_call(
+    inward = (extra * strip // PIECE, 2, MEMBERS, PIECE, channels)
+    outward = (chunks, 2, MEMBERS, BATCH, channels)
+    results, grad_qkv, grad_out = pl.pallas_call(
         functools.partial(kernel, plan),
         out_shape=(
-            jax.ShapeDtypeStruct(shape, BF16),
-            jax.ShapeDtypeStruct(shape, BF16),
+            jax.ShapeDtypeStruct((2,) + shape, BF16),
             jax.ShapeDtypeStruct((channels, 3 * channels), F32),
             jax.ShapeDtypeStruct((channels, channels), F32),
         ),
         in_specs=[anywhere, anywhere] + [vmem] * 7,
-        out_specs=(anywhere, anywhere, vmem, vmem),
+        out_specs=(anywhere, vmem, vmem),
         scratch_shapes=[
-            pltpu.VMEM(box, BF16),
-            pltpu.VMEM(box, BF16),
+            pltpu.VMEM(inward, BF16),
+            pltpu.VMEM(outward, BF16),
             pltpu.VMEM((channels, 4 * channels), F32),
             pltpu.VMEM((channels // 128, rows, 128), F32),
             pltpu.VMEM((rows, channels), BF16),
@@ -423,8 +430,7 @@
             dma((row_devices,)),
             dma((row_devices,)),
             dma((column_devices,)),
-            dma((chunks,)),
-            dma(()),
+            dma((inward[0],)),
             dma(()),
             dma((4,)),
         ],
@@ -443,8 +449,8 @@
         w_down,
     )
     return (
-        mixed.reshape(tokens.shape),
-        grad_tokens.reshape(tokens.shape),
+        results[0].reshape(tokens.shape),
+        results[1].reshape(tokens.shape),
         grad_qkv,
         grad_out,
     )

time: 206 us -> 217 us (1.053); the launches traced: 203 us -> 216 us
  Pallas kernels: 196 us -> 209 us
    pallas_call x1, Pallas kernels: 196 us -> 209 us  [local(): pl.pallas_call(functools.partial(kernel, plan), out_shape=(jax.ShapeDtype...]
    unnamed x10 -> x6, local copies, waits for them, and re-layouts: 6.54 us -> 1.59 us
    slice x0 -> x1, local copies, waits for them, and re-layouts: none -> 4.9 us  [local(): results[1].reshape(tokens.shape)]
where the time goes in v5:
time: 217 us; the launch traced here: 216 us
  Pallas kernels  209 us (96%)
  local copies, waits for them, and re-layouts  6.5 us (3%)
    pallas_call x1, Pallas kernels, local(): pl.pallas_call(functools.partial(kernel, plan), out_shape=(jax.ShapeDtype...  209 us
    slice x1, local copies, waits for them, and re-layouts, local(): results[1].reshape(tokens.shape)  4.9 us

profile of v5, /device:TPU:25, one launch (start us, length us, event | category | flops | bytes accessed | tf_op | source)
XLA Modules:
  0.0 216.2 jit_solution(2556448254219872007)
XLA Ops:
  0.6 209.0 %shard_map.120 = (bf16[2,32,2,64,256]{4,3,2,1,0:T(8,128)(2,1)}, f32[256,768]{1,0:T(8,128)}, f32[256,256]{1,0:T(8,128)}) custom-call(bf16[32,2,64,256]{3,2,1,0:T(8,128)(2,1)} %bitcast.7, bf16[32,2,64,256]{3,2,1,0:T(8,128)(2,1)} %bitcast.8, f32[1,256]{1,0:T(1,128)} %bitcast.12, bf16[256,768]{1,0:T(8,128)(2,1)} %w_qkv.1, bf16[256,256]{1,0:T(8,128)(2,1)} %w_out.1, ...), custom_call_target="tpu_custom_call" | custom-call | tf_op jit(solution)/shard_map/pallas_call | solution.py:397
  209.7 0.0 copy-start
  209.7 0.0 copy-start.1
  209.7 4.9 %fusion = (bf16[1,32,2,64,256]{4,3,2,1,0:T(8,128)(2,1)}, bf16[1,32,2,64,256]{4,3,2,1,0:T(8,128)(2,1)}) fusion(bf16[2,32,2,64,256]{4,3,2,1,0:T(8,128)(2,1)} %get-tuple-element.7), kind=kLoop, calls=%fused_computation | loop fusion | bytes 8388608 | tf_op jit(solution)/shard_map/slice | solution.py:453
  214.6 0.0 copy-done
  214.6 0.9 copy.15
  215.5 0.0 copy-done.1
  215.5 0.7 copy.16
Async XLA Ops:
  209.7 4.9 %copy-start = (f32[256,768]{1,0:T(8,128)S(1)}, f32[256,768]{1,0:T(8,128)}, u32[]{:S(2)}) copy-start(f32[256,768]{1,0:T(8,128)} %get-tuple-element.18) | copy-start | bytes 2359300
  209.7 5.8 %copy-start.1 = (f32[256,256]{1,0:T(8,128)S(1)}, f32[256,256]{1,0:T(8,128)}, u32[]{:S(2)}) copy-start(f32[256,256]{1,0:T(8,128)} %get-tuple-element.19) | copy-start | bytes 786436

commit v6 on v4

--- a/solution.py
+++ b/solution.py
@@ -316,10 +316,10 @@
             for column, row, top, left in areas():
                 parts[column, row] = acc[top : top + height, left : left + width].astype(BF16)
             exchange(0, 1, lambda other: parts.at[other], column_parts, sent_column)
-            send_home(chunks - 2, 1)
+            send_home(chunks - 2, 0)
 
         mlp()
-        send_home(chunk, 0)
+        pl.when(chunk < chunks - 2)(lambda: send_home(chunk, 0))
         token_gradient()
         pl.when(chunk < chunks - 2)(lambda: send_home(chunk, 1))
         return _
@@ -329,12 +329,14 @@
     arrive(0, column_parts)
     column_sum[...] = jnp.sum(column_parts[...].astype(F32), axis=0).astype(BF16)
     exchange(1, 0, lambda other: column_sum.at[other], row_parts, sent_row)
+    send_home(chunks - 2, 1)
     arrive(1, row_parts)
     share[...] = jnp.sum(row_parts[...].astype(F32), axis=0).astype(BF16)
     exchange(2, 0, lambda other: share, row_shares, sent_row_back)
-    send_home(chunks - 1, 1)
+    send_home(chunks - 1, 0)
     arrive(2, row_shares)
     exchange(3, 1, lambda other: row_shares, shares, sent_column_back)
+    send_home(chunks - 1, 1)
     arrive(3, shares)
     for column, row, top, left in areas():
         value = shares[column, row].astype(F32) * factor

time: 206 us -> 202 us (0.981); the launches traced: 203 us -> 202 us
  no operation moved by 1% of the time
where the time goes in v6:
time: 202 us
  Pallas kernels  194 us (96%)
  local copies, waits for them, and re-layouts  6.54 us (3%)
    pallas_call x1, Pallas kernels, local(): pl.pallas_call(functools.partial(kernel, plan), out_shape=(jax.ShapeDtype...  194 us
    unnamed x10, local copies, waits for them, and re-layouts  6.54 us

profile of v6, /device:TPU:25, one launch (start us, length us, event | category | flops | bytes accessed | tf_op | source)
XLA Modules:
  0.0 201.6 jit_solution(13277485403512369279)
XLA Ops:
  0.6 194.4 %shard_map.120 = (bf16[32,2,64,256]{3,2,1,0:T(8,128)(2,1)}, bf16[32,2,64,256]{3,2,1,0:T(8,128)(2,1)}, f32[256,768]{1,0:T(8,128)}, f32[256,256]{1,0:T(8,128)}) custom-call(bf16[32,2,64,256]{3,2,1,0:T(8,128)(2,1)} %bitcast.7, bf16[32,2,64,256]{3,2,1,0:T(8,128)(2,1)} %bitcast.8, f32[1,256]{1,0:T(1,128)} %bitcast.12, bf16[256,768]{1,0:T(8,128)(2,1)} %w_qkv.1, ...), custom_call_target="tpu_custom_call" | custom-call | tf_op jit(solution)/shard_map/pallas_call | solution.py:391
  195.0 0.0 copy-start
  195.0 3.3 %copy.17 = bf16[32,128,256]{2,1,0:T(8,128)(2,1)} copy(bf16[32,128,256]{2,1,0:T(8,128)(2,1)} %bitcast.10) | data formatting | bytes 4194304
  198.3 0.0 copy-done
  198.3 0.0 copy-start.1
  198.3 0.0 copy-start.2
  198.3 1.3 copy.18
  199.6 0.4 copy-done.1
  200.0 0.9 copy.19
  200.8 0.0 copy-done.2
  200.8 0.7 copy.20
Async XLA Ops:
  195.0 3.3 %copy-start = (bf16[32,2,64,256]{3,2,1,0:T(8,128)(2,1)S(1)}, bf16[32,2,64,256]{3,2,1,0:T(8,128)(2,1)}, u32[]{:S(2)}) copy-start(bf16[32,2,64,256]{3,2,1,0:T(8,128)(2,1)} %get-tuple-element.9) | copy-start | bytes 6291460
  198.3 1.7 copy-start.1
  198.3 2.6 %copy-start.2 = (f32[256,256]{1,0:T(8,128)S(1)}, f32[256,256]{1,0:T(8,128)}, u32[]{:S(2)}) copy-start(f32[256,256]{1,0:T(8,128)} %get-tuple-element.19) | copy-start | bytes 786436

commit v7 on v6

--- a/solution.py
+++ b/solution.py
@@ -316,10 +316,9 @@
             for column, row, top, left in areas():
                 parts[column, row] = acc[top : top + height, left : left + width].astype(BF16)
             exchange(0, 1, lambda other: parts.at[other], column_parts, sent_column)
-            send_home(chunks - 2, 0)
 
         mlp()
-        pl.when(chunk < chunks - 2)(lambda: send_home(chunk, 0))
+        pl.when(chunk < chunks - 1)(lambda: send_home(chunk, 0))
         token_gradient()
         pl.when(chunk < chunks - 2)(lambda: send_home(chunk, 1))
         return _

time: 202 us -> 203 us (level)
  no operation moved by 1% of the time
where the time goes in v7:
time: 203 us; the launch traced here: 202 us
  Pallas kernels  194 us (96%)
  local copies, waits for them, and re-layouts  6.54 us (3%)
    pallas_call x1, Pallas kernels, local(): pl.pallas_call(functools.partial(kernel, plan), out_shape=(jax.ShapeDtype...  194 us
    unnamed x10, local copies, waits for them, and re-layouts  6.54 us

profile of v7, /device:TPU:25, one launch (start us, length us, event | category | flops | bytes accessed | tf_op | source)
XLA Modules:
  0.0 201.6 jit_solution(10431490786226741567)
XLA Ops:
  0.6 194.4 %shard_map.120 = (bf16[32,2,64,256]{3,2,1,0:T(8,128)(2,1)}, bf16[32,2,64,256]{3,2,1,0:T(8,128)(2,1)}, f32[256,768]{1,0:T(8,128)}, f32[256,256]{1,0:T(8,128)}) custom-call(bf16[32,2,64,256]{3,2,1,0:T(8,128)(2,1)} %bitcast.7, bf16[32,2,64,256]{3,2,1,0:T(8,128)(2,1)} %bitcast.8, f32[1,256]{1,0:T(1,128)} %bitcast.12, bf16[256,768]{1,0:T(8,128)(2,1)} %w_qkv.1, ...), custom_call_target="tpu_custom_call" | custom-call | tf_op jit(solution)/shard_map/pallas_call | solution.py:390
  195.0 0.0 copy-start
  195.0 3.3 %copy.17 = bf16[32,128,256]{2,1,0:T(8,128)(2,1)} copy(bf16[32,128,256]{2,1,0:T(8,128)(2,1)} %bitcast.10) | data formatting | bytes 4194304
  198.3 0.0 copy-done
  198.3 0.0 copy-start.1
  198.3 0.0 copy-start.2
  198.3 1.3 copy.18
  199.6 0.4 copy-done.1
  200.0 0.9 copy.19
  200.8 0.0 copy-done.2
  200.9 0.7 copy.20
Async XLA Ops:
  195.0 3.3 %copy-start = (bf16[32,2,64,256]{3,2,1,0:T(8,128)(2,1)S(1)}, bf16[32,2,64,256]{3,2,1,0:T(8,128)(2,1)}, u32[]{:S(2)}) copy-start(bf16[32,2,64,256]{3,2,1,0:T(8,128)(2,1)} %get-tuple-element.9) | copy-start | bytes 6291460
  198.3 1.7 copy-start.1
  198.3 2.6 %copy-start.2 = (f32[256,256]{1,0:T(8,128)S(1)}, f32[256,256]{1,0:T(8,128)}, u32[]{:S(2)}) copy-start(f32[256,256]{1,0:T(8,128)} %get-tuple-element.19) | copy-start | bytes 786436
